TPU v7x, 256 devices: a whole 4x4x8 slice. The times are simulated.
256 devices in a mesh: coal: 8 (over z_lo, core), section: 4 (over y), tensor: 8 (over x, z_hi).
Axes of the slice: x: 4, y: 4, z: 8 (z_hi: 2, z_lo: 4; z = z_hi * 4 + z_lo), core: 2. Of those that a mesh axis runs over, the one named last changes fastest.
Arguments:
- hidden: bfloat16 [32, 128, 8192], P('coal', None, 'section'), parts along dimension 0, may hold values from -120 to 120
- norm_gain: float32 [8192], P('section'), may hold values from 0.1 to 1.9
- w_query: bfloat16 [8192, 8192], P('section', 'tensor'), may hold values from -0.0625 to 0.0625
- w_key: bfloat16 [8192, 1024], P('section', 'tensor'), may hold values from -0.0625 to 0.0625
- w_value: bfloat16 [8192, 1024], P('section', 'tensor'), may hold values from -0.0625 to 0.0625
- w_out: bfloat16 [8192, 8192], P('tensor', 'section'), may hold values from -0.0625 to 0.0625
- cache_key: bfloat16 [8192, 1024], P('section', 'tensor'), may hold values from -400 to 400
- cache_value: bfloat16 [8192, 1024], P('section', 'tensor'), may hold values from -6 to 6
- block_mask: int32 [32, 128], P('coal'), parts along dimension 0, may hold values from 0 to 1
Outputs:
- attn_out: bfloat16 [32, 128, 8192], P('coal', None, ('section', 'tensor')), parts along dimension 0
There are 8 independent parts, one for each index of `coal`. A program takes and returns all parts, laid end to end along the dimension named above; an argument that names none is the same for every part. Nothing has to cross between parts.
All inputs are finite; a program needn't handle non-finite values.
Results may differ from a plain program's by a relative error of at most 0.015.
Values may be sent and summed in bfloat16 or wider, within the bound.
No kernel may reach another device: no remote copies, remote signals or barrier semaphores. Data moves between devices by JAX's collectives and lax.ppermute only.
A program may use at most 128 MiB of HBM per device.

v0:
```python
import functools
import math

import jax
import jax.numpy as jnp
from jax import lax
from jax.experimental import pallas as pl
from jax.experimental.pallas import tpu as pltpu
from jax.sharding import PartitionSpec as P

D = 8192
HD = 128
NBLK = 128
BLOCK = 64
rope_base = 500000.0
norm_eps = 1e-05
masked_score = -1e30
BF = jnp.bfloat16
F32 = jnp.float32
HALVES = 2
TILE = 1024
MIB = 1024 * 1024


def section_shift(x, by):
    n = lax.axis_size("section")
    return lax.ppermute(x, "section", [(i, (i + by) % n) for i in range(n)])


def x_shift(x, by):
    n = lax.axis_size("tensor") // 2
    return lax.ppermute(
        x, "tensor", [(i, ((i // 2 + by) % n) * 2 + i % 2) for i in range(2 * n)]
    )


def z_swap(x):
    return lax.ppermute(x, "tensor", [(i, i ^ 1) for i in range(lax.axis_size("tensor"))])


def core_swap(x):
    return lax.ppermute(x, "coal", [(i, i ^ 1) for i in range(lax.axis_size("coal"))])


def project_kernel(place, hidden, gain, w_query, w_key, w_value, *rest):
    outs, (rows, weights, scaled, product, sem) = rest[:-5], rest[-5:]
    count, answer, width = hidden.shape
    queries = w_query.shape[1]
    span = answer // HALVES
    steps, _, _, depth = rows.shape
    copies = []
    for k in range(steps):
        at = pl.ds(k * depth, depth)
        group = [
            (hidden.at[lax.rem(place[0] + r, count), :, at], rows.at[k, r]) for r in range(count)
        ]
        group += [
            (w_query.at[at], weights.at[at, pl.ds(0, queries)]),
            (w_key.at[at], weights.at[at, pl.ds(queries, HD)]),
            (w_value.at[at], weights.at[at, pl.ds(queries + HD, HD)]),
        ]
        copies.append(
            [pltpu.make_async_copy(a, b, sem.at[k, i]) for i, (a, b) in enumerate(group)]
        )
        for copy in copies[-1]:
            copy.start()

    squares = [jnp.zeros((answer, 128), F32) for _ in range(count)]
    for k in range(steps):
        at = slice(k * depth, (k + 1) * depth)
        for copy in copies[k]:
            copy.wait()
        for r in range(count):
            x = rows[k, r].astype(F32)
            x2 = x * x
            for j in range(depth // 128):
                squares[r] = squares[r] + x2[:, j * 128 : (j + 1) * 128]
            scaled[k, r * answer : (r + 1) * answer] = (x * gain[:, at]).astype(BF)
        partial = jnp.dot(scaled[k], weights[at], preferred_element_type=F32)
        if k == 0:
            product[...] = partial
        elif k < steps - 1:
            product[...] += partial
        else:
            partial = product[...] + partial
            lane = lax.broadcasted_iota(jnp.int32, (answer, 128), 1)
            for r in range(count):
                total = jnp.sum(squares[r], axis=-1, keepdims=True)
                high = total.astype(BF).astype(F32)
                pair = jnp.where(lane == 0, high, jnp.where(lane == 1, total - high, 0.0))
                for h in range(HALVES):
                    out = outs[r * HALVES + h]
                    start = r * answer + h * span
                    out[:, : queries + 2 * HD] = partial[start : start + span].astype(BF)
                    out[:, queries + 2 * HD :] = pair[h * span : (h + 1) * span].astype(BF)


def project(place, hidden, gain, w_query, w_key, w_value):
    count, answer, width = hidden.shape
    total = w_query.shape[1] + 2 * HD
    steps = 4
    smem = pl.BlockSpec(memory_space=pltpu.SMEM)
    vmem = pl.BlockSpec(memory_space=pltpu.VMEM)
    anywhere = pl.BlockSpec(memory_space=pl.ANY)
    return pl.pallas_call(
        project_kernel,
        in_specs=[smem, anywhere, vmem, anywhere, anywhere, anywhere],
        out_specs=[vmem] * (count * HALVES),
        out_shape=[jax.ShapeDtypeStruct((answer // HALVES, total + HD), BF)] * (count * HALVES),
        scratch_shapes=[
            pltpu.VMEM((steps, count, answer, width // steps), BF),
            pltpu.VMEM((width, total), BF),
            pltpu.VMEM((steps, count * answer, width // steps), BF),
            pltpu.VMEM((count * answer, total), F32),
            pltpu.SemaphoreType.DMA((steps, count + 3)),
        ],
        compiler_params=pltpu.CompilerParams(vmem_limit_bytes=60 * MIB),
        cost_estimate=pl.CostEstimate(
            flops=2 * count * answer * width * total, bytes_accessed=9 * MIB, transcendentals=0
        ),
        name="project",
    )(place, hidden, gain, w_query, w_key, w_value)


def attention_kernel(half, place, mask, p0, p1, p2, p3, cosine, sine, *rest):
    before, rest = (rest[:2], rest[2:]) if half else ((), rest)
    own_key, own_value, a1, b1, a3, b3, key2, value2, key2b, value2b, out, *rest = rest
    after, rest = ([], rest) if half == HALVES - 1 else (rest[:2], rest[2:])
    queries, near_key, near_value, keys, values, buf0, buf1, sem = rest
    section, core = place[0], place[1]
    span = p0.shape[0]
    answer = near_key.shape[0]
    heads = out.shape[1] // HD
    rows = heads * span
    local = own_key.shape[0]
    piece_rows = local // 2
    sections = keys.shape[0] // local

    copies = []

    def bring(source, buffer, start, size):
        copy = pltpu.make_async_copy(
            source,
            buffer.at[pl.ds(pl.multiple_of(start, size), size), pl.ds(0, HD)],
            sem.at[len(copies)],
        )
        copy.start()
        copies.append(copy)

    bring(own_key, keys, section * local, local)
    bring(own_value, values, section * local, local)
    pairs = [(r, p.at[0], p.at[1]) for r, p in ((1, a1), (1, b1), (3, a3), (3, b3))]
    pairs += [(2, key2, value2), (2, key2b, value2b)]
    for n, (r, *pair) in enumerate(pairs):
        source = lax.rem(section + sections - r, sections)
        side = core if n % 2 == 0 else 1 - core
        for piece, buffer in zip(pair, (keys, values)):
            bring(piece, buffer, source * local + side * piece_rows, piece_rows)

    first = jnp.where(lax.broadcasted_iota(jnp.int32, (rows, HD), 1) == 0, 1.0, 0.0).astype(BF)

    def fill(b, carry):
        at = pl.ds(pl.multiple_of(b * BLOCK, BLOCK), BLOCK)
        bias = jnp.where(mask[section, b] > 0, 0.0, masked_score)
        keys[at, HD:] = jnp.full((BLOCK, HD), bias, F32).astype(BF)
        values[at, HD:] = first[:BLOCK]
        return carry

    lax.fori_loop(0, keys.shape[0] // BLOCK, fill, 0, unroll=4)

    width = (heads + 2) * HD
    total = (
        p0[:, width:].astype(F32) + p1[:, width:].astype(F32)
        + p2[:, width:].astype(F32) + p3[:, width:].astype(F32)
    )
    scale = lax.rsqrt((total[:, 0:1] + total[:, 1:2]) / D + norm_eps)

    def column(h):
        at = slice(h * HD, (h + 1) * HD)
        return (
            p0[:, at].astype(F32) + p1[:, at].astype(F32)
            + p2[:, at].astype(F32) + p3[:, at].astype(F32)
        ) * scale

    def turned(x):
        return x * cosine[...] + pltpu.roll(x, HD // 2, 1) * sine[...]

    factor = math.log2(math.e) / math.sqrt(HD)
    for h in range(heads):
        queries[h * span : (h + 1) * span] = (turned(column(h)) * factor).astype(BF)
    new_key = turned(column(heads)).astype(BF)
    new_value = column(heads + 1).astype(BF)
    for ref, new in zip(after, (new_key, new_value)):
        ref[...] = new
    near_value[:, HD:] = first[:answer]
    for h in range(HALVES):
        at = slice(h * span, (h + 1) * span)
        if h == half:
            near_key[at], near_value[at, :HD] = new_key, new_value
        elif h < half:
            near_key[at], near_value[at, :HD] = before[0][...], before[1][...]
        else:
            near_key[at] = jnp.zeros((span, HD), BF)
            near_value[at, :HD] = jnp.zeros((span, HD), BF)

    tile = buf0.shape[1]
    tiles = keys.shape[0] // tile
    dims = (((1,), (1,)), ((), ()))
    q = queries[...]
    q_aug = jnp.concatenate([q, first], axis=1)
    s = lax.dot_general(q, near_key[...], dims, preferred_element_type=F32)
    row = lax.rem(lax.broadcasted_iota(jnp.int32, (rows, answer), 0), span) + half * span
    s = jnp.where(row >= lax.broadcasted_iota(jnp.int32, (rows, answer), 1), s, masked_score)
    m = jnp.max(s, axis=-1, keepdims=True)
    acc = jnp.dot(jnp.exp2(s - m).astype(BF), near_value[...], preferred_element_type=F32)

    for copy in copies:
        copy.wait()

    def score(t, buffer):
        at = pl.ds(pl.multiple_of(t * tile, tile), tile)
        s = lax.dot_general(q_aug, keys[at], dims, preferred_element_type=F32)
        buffer[...] = s
        return jnp.max(s, axis=-1, keepdims=True)

    def weigh(t, buffer, m, m_new, acc):
        at = pl.ds(pl.multiple_of(t * tile, tile), tile)
        p = jnp.exp2(buffer[...] - m_new).astype(BF)
        return acc * jnp.exp2(m - m_new) + jnp.dot(p, values[at], preferred_element_type=F32)

    def pair(i, state):
        m, top, acc = state
        t = 2 * i
        m_new = jnp.maximum(m, top)
        top = score(t + 1, buf1)
        acc = weigh(t, buf0, m, m_new, acc)
        m = m_new
        m_new = jnp.maximum(m, top)
        top = score(lax.rem(t + 2, tiles), buf0)
        acc = weigh(t + 1, buf1, m, m_new, acc)
        return m_new, top, acc

    m, _, acc = lax.fori_loop(0, tiles // 2, pair, (m, score(0, buf0), acc))
    result = (acc[:, :HD] / acc[:, HD : HD + 1]).astype(BF)
    for h in range(heads):
        out[:, h * HD : (h + 1) * HD] = result[h * span : (h + 1) * span]


def attend(half, place, mask, parts, cosine, sine, before, own_key, own_value, pieces):
    span = parts[0].shape[0]
    answer = span * HALVES
    context = NBLK * BLOCK
    heads = parts[0].shape[1] // HD - 3
    rows = heads * span
    vmem = pl.BlockSpec(memory_space=pltpu.VMEM)
    smem = pl.BlockSpec(memory_space=pltpu.SMEM)
    anywhere = pl.BlockSpec(memory_space=pl.ANY)
    extra = 0 if half == HALVES - 1 else 2
    outs = [jax.ShapeDtypeStruct((span, heads * HD), BF)]
    outs += [jax.ShapeDtypeStruct((span, HD), BF)] * extra
    return pl.pallas_call(
        functools.partial(attention_kernel, half),
        in_specs=[smem, smem] + [vmem] * (6 + len(before)) + [anywhere] * 10,
        out_specs=[vmem] * (1 + extra),
        out_shape=outs,
        scratch_shapes=[
            pltpu.VMEM((rows, HD), BF),
            pltpu.VMEM((answer, HD), BF),
            pltpu.VMEM((answer, 2 * HD), BF),
            pltpu.VMEM((context, 2 * HD), BF),
            pltpu.VMEM((context, 2 * HD), BF),
            pltpu.VMEM((rows, TILE), F32),
            pltpu.VMEM((rows, TILE), F32),
            pltpu.SemaphoreType.DMA((14,)),
        ],
        compiler_params=pltpu.CompilerParams(vmem_limit_bytes=32 * MIB),
        cost_estimate=pl.CostEstimate(
            flops=8 * rows * context * HD,
            bytes_accessed=6 * MIB,
            transcendentals=rows * context,
        ),
        name="attend",
    )(place, mask, *parts, cosine, sine, *before, own_key, own_value, *pieces)


def output_kernel(place, a0, a1, a2, a3, w_out, before, o0, o1, o2, o3, after, rows, weights, sem):
    count, span, depth = rows.shape
    outs = (o0, o1, o2, o3)
    after[...] = jnp.zeros_like(after)
    width = w_out.shape[1] // len(outs)
    copies = []
    for k in range(len(outs)):
        at = pl.ds(pl.multiple_of(lax.rem(place[2] + k, len(outs)) * width, width), width)
        copies.append(pltpu.make_async_copy(w_out.at[:, at], weights.at[k], sem.at[k]))
        copies[-1].start()
    for r, part in enumerate((a0, a1, a2, a3)):
        rows[lax.rem(place[0] + count - r, count)] = part[...]
    left = rows[...].reshape(count * span, depth)
    for k, out in enumerate(outs):
        copies[k].wait()
        for side in range(2):
            at = slice(side * width // 2, (side + 1) * width // 2)
            out[side] = jnp.dot(left, weights[k, :, at], preferred_element_type=F32).astype(
                out.dtype
            )


def project_out(place, parts, w_out, before):
    span, depth = parts[0].shape
    count = len(parts)
    width = w_out.shape[1] // 4
    vmem = pl.BlockSpec(memory_space=pltpu.VMEM)
    smem = pl.BlockSpec(memory_space=pltpu.SMEM)
    shape = (2, count * span, width // 2)
    return pl.pallas_call(
        output_kernel,
        in_specs=[smem] + [vmem] * count + [pl.BlockSpec(memory_space=pl.ANY)] * 2,
        out_specs=[vmem] * 5,
        out_shape=[jax.ShapeDtypeStruct(shape, F32)]
        + [jax.ShapeDtypeStruct(shape, BF)] * 3
        + [jax.ShapeDtypeStruct((8, 128), F32)],
        scratch_shapes=[
            pltpu.VMEM((count, span, depth), BF),
            pltpu.VMEM((4, depth, width), BF),
            pltpu.SemaphoreType.DMA((4,)),
        ],
        compiler_params=pltpu.CompilerParams(vmem_limit_bytes=24 * MIB),
        cost_estimate=pl.CostEstimate(
            flops=8 * count * span * depth * width, bytes_accessed=6 * MIB, transcendentals=0
        ),
        name="project_out",
    )(place, *parts, w_out, before)


def reduce_kernel(place, before, *refs):
    pieces, (send, keep) = refs[:-2], refs[-2:]
    for side, out in ((1 - place[3], send), (place[3], keep)):
        total = pieces[0][side].astype(F32)
        for piece in pieces[1:]:
            total = total + piece[side].astype(F32)
        out[...] = total.astype(out.dtype)


def reduce_pieces(place, before, pieces):
    _, rows, width = pieces[0].shape
    vmem = pl.BlockSpec(memory_space=pltpu.VMEM)
    return pl.pallas_call(
        reduce_kernel,
        in_specs=[pl.BlockSpec(memory_space=pltpu.SMEM), pl.BlockSpec(memory_space=pl.ANY)]
        + [vmem] * len(pieces),
        out_specs=[vmem] * 2,
        out_shape=[jax.ShapeDtypeStruct((rows, width), t) for t in (BF, F32)],
        compiler_params=pltpu.CompilerParams(vmem_limit_bytes=16 * MIB),
        cost_estimate=pl.CostEstimate(flops=8 * rows * width, bytes_accessed=16 * rows * width, transcendentals=0),
        name="reduce_pieces",
    )(place, before, *pieces)


def finish_kernel(earlier, keep, arrived, out):
    count, rows, _ = out.shape
    start = earlier.shape[1]
    out[:, :start] = earlier[...]
    total = (keep[...] + arrived[...].astype(F32)).astype(out.dtype)
    for c in range(count):
        out[c, start:] = total[c * (rows - start) : (c + 1) * (rows - start)]


def finish(earlier, keep, arrived):
    count, rows, width = earlier.shape
    vmem = pl.BlockSpec(memory_space=pltpu.VMEM)
    return pl.pallas_call(
        finish_kernel,
        in_specs=[vmem] * 3,
        out_specs=vmem,
        out_shape=jax.ShapeDtypeStruct((count, rows + keep.shape[0] // count, width), BF),
        compiler_params=pltpu.CompilerParams(vmem_limit_bytes=16 * MIB),
        name="finish",
    )(earlier, keep, arrived)


def rotation(answer):
    half = HD // 2
    positions = (NBLK * BLOCK + jnp.arange(answer)).astype(F32)
    frequency = rope_base ** (-2.0 * jnp.arange(half).astype(F32) / HD)
    angles = positions[:, None] * frequency[None, :]
    cosine, sine = jnp.cos(angles), jnp.sin(angles)
    return jnp.concatenate([cosine, cosine], axis=1), jnp.concatenate([-sine, sine], axis=1)


def per_device(
    hidden, norm_gain, w_query, w_key, w_value, w_out, cache_key, cache_value, block_mask
):
    section = lax.axis_index("section")
    core = lax.rem(lax.axis_index("coal"), 2)
    tensor = lax.axis_index("tensor")
    z_hi = lax.rem(tensor, 2)
    place = jnp.stack([section, core, tensor // 2, z_hi]).astype(jnp.int32)
    answer = hidden.shape[1]
    span = answer // HALVES
    half_rows = cache_key.shape[0] // 2
    piece = jnp.stack(
        [
            lax.dynamic_slice_in_dim(cache_key, core * half_rows, half_rows, 0),
            lax.dynamic_slice_in_dim(cache_value, core * half_rows, half_rows, 0),
        ]
    )
    with jax.named_scope("cache"):
        mine1, mine3 = section_shift(piece, 1), section_shift(piece, 3)
    with jax.named_scope("forward"):
        key2, value2 = section_shift(mine1[0], 1), section_shift(mine3[1], 3)
    with jax.named_scope("swap"):
        pieces = (mine1, core_swap(mine1), mine3, core_swap(mine3))
        pieces += (key2, value2, core_swap(key2), core_swap(value2))
    cosine, sine = rotation(answer)

    chunks = project(place, hidden, norm_gain[None, :], w_query, w_key, w_value)
    parts = []
    for h in range(HALVES):
        with jax.named_scope(f"sums{h}"):
            parts.append(
                [chunks[h]] + [section_shift(chunks[r * HALVES + h], r) for r in (1, 2, 3)]
            )
    before, attended, gathered = [], [], []
    for h in range(HALVES):
        at = slice(h * span, (h + 1) * span)
        attention, *before = attend(
            h, place, block_mask, parts[h], cosine[at], sine[at], before,
            cache_key, cache_value, pieces,
        )
        attended.append(attention)
        with jax.named_scope(f"gather{h}"):
            gathered.append([attention] + [section_shift(attention, r) for r in (1, 2, 3)])

    turn, send = attended[-1], attended[0]
    for h in range(HALVES):
        *sums, turn = project_out(place, gathered[h], w_out, turn)
        with jax.named_scope(f"x{h}"):
            pieces = [sums[0]] + [x_shift(sums[r], r) for r in (1, 2, 3)]
        send, keep = reduce_pieces(place, send, pieces)
        with jax.named_scope(f"z{h}"):
            arrived = z_swap(send)
        if h == 0:
            result = (keep + arrived.astype(F32)).astype(BF)
            result = result.reshape(hidden.shape[0], answer // HALVES, -1)
        else:
            result = finish(result, keep, arrived)
    return result


def solution(mesh):
    return jax.shard_map(
        per_device,
        mesh=mesh,
        in_specs=(
            P("coal", None, "section"),
            P("section"),
            P("section", "tensor"),
            P("section", "tensor"),
            P("section", "tensor"),
            P("tensor", "section"),
            P("section", "tensor"),
            P("section", "tensor"),
            P("coal", None),
        ),
        out_specs=P("coal", None, ("section", "tensor")),
        check_vma=False,
    )
```

profile of v0, /device:TPU:34, one launch (start us, length us, event | category | flops | bytes accessed | tf_op | source)
XLA Modules:
  0.0 110.0 jit_solution(15477071531718297576)
XLA Ops:
  0.0 1.1 dynamic-slice_bitcast_fusion
  1.1 0.1 pad_maximum_fusion
  1.1 1.7 %collective-permute-start.3 = (bf16[2,1024,128]{2,1,0:T(8,128)(2,1)S(1)}, bf16[2,1024,128]{2,1,0:T(8,128)(2,1)S(1)}, u32[]{:S(2)}, u32[]{:S(2)}) collective-permute-start(bf16[2,1024,128]{2,1,0:T(8,128)(2,1)S(1)} %pad_maximum_fusion), channel_id=1, source_target_pairs={{0,8},{8,16},{16,24},{24,0},{1,9},{9,17},{17,25},{25,1},{2,10},{10... | collective-permute-start | bytes 1572872 | tf_op jit(solution)/shard_map/cache/ppermute | solution.py:27
  2.8 1.7 %collective-permute-start.5 = (bf16[2,1024,128]{2,1,0:T(8,128)(2,1)S(1)}, bf16[2,1024,128]{2,1,0:T(8,128)(2,1)S(1)}, u32[]{:S(2)}, u32[]{:S(2)}) collective-permute-start(bf16[2,1024,128]{2,1,0:T(8,128)(2,1)S(1)} %pad_maximum_fusion), channel_id=1, source_target_pairs={{0,24},{8,0},{16,8},{24,16},{1,25},{9,1},{17,9},{25,17},{2,26},{10... | collective-permute-start | bytes 1572872 | tf_op jit(solution)/shard_map/cache/ppermute | solution.py:27
  4.4 0.7 pad_add_fusion.place
  5.1 7.5 %project.1 = (bf16[64,1408]{1,0:T(8,128)(2,1)}, bf16[64,1408]{1,0:T(8,128)(2,1)}, bf16[64,1408]{1,0:T(8,128)(2,1)}, bf16[64,1408]{1,0:T(8,128)(2,1)}, bf16[64,14...) custom-call(s32[4]{0:T(128)} %pad_add_fusion.place, ...), custom_call_target="tpu_custom_call" | custom-call | flops 2684354560 | bytes 9437184 | tf_op jit(solution)/shard_map/project/pallas_call | solution.py:105
  12.6 0.4 collective-permute-start
  13.1 3.1 %collective-permute-done.3.rest_2_.rest_4_ = bf16[2,1024,128]{2,1,0:T(8,128)(2,1)S(1)} collective-permute-done((bf16[2,1024,128]{2,1,0:T(8,128)(2,1)S(1)}, bf16[2,1024,128]{2,1,0:T(8,128)(2,1)S(1)}, u32[]{:S(2)}, u32[]{:S(2)}) %collective-permute-start.3) | collective-permute-done | bytes 524320 | tf_op jit(solution)/shard_map/cache/ppermute | solution.py:27
  16.2 1.5 %collective-permute-start.7 = (bf16[1024,128]{1,0:T(8,128)(2,1)S(1)}, bf16[1024,128]{1,0:T(8,128)(2,1)S(1)}, u32[]{:S(2)}, u32[]{:S(2)}) collective-permute-start(bf16[1024,128]{1,0:T(8,128)(2,1)S(1)} %slice_bitcast_fusion.1), channel_id=1, source_target_pairs={{0,8},{8,16},{16,24},{24,0},{1,9},{9,17},{17,25},{25,1},{2,10},{10... | collective-permute-start | bytes 786440 | tf_op jit(solution)/shard_map/forward/ppermute | solution.py:27
  17.7 0.0 collective-permute-done.5.rest_4_.rest_6_
  17.7 1.9 %collective-permute-start.8 = (bf16[1024,128]{1,0:T(8,128)(2,1)S(1)}, bf16[1024,128]{1,0:T(8,128)(2,1)S(1)}, u32[]{:S(2)}, u32[]{:S(2)}) collective-permute-start(bf16[1024,128]{1,0:T(8,128)(2,1)S(1)} %slice_bitcast_fusion), channel_id=1, source_target_pairs={{0,24},{8,0},{16,8},{24,16},{1,25},{9,1},{17,9},{25,17},{2,26},{10... | collective-permute-start | bytes 786440 | tf_op jit(solution)/shard_map/forward/ppermute | solution.py:27
  19.6 1.9 %collective-permute-start.1 = (bf16[64,1408]{1,0:T(8,128)(2,1)}, bf16[64,1408]{1,0:T(8,128)(2,1)S(1)}, u32[]{:S(2)}, u32[]{:S(2)}) collective-permute-start(bf16[64,1408]{1,0:T(8,128)(2,1)} %get-tuple-element.31), channel_id=1, source_target_pairs={{0,16},{8,24},{16,0},{24,8},{1,17},{9,25},{17,1},{25,9},{2,18},{10... | collective-permute-start | bytes 540680 | tf_op jit(solution)/shard_map/sums0/ppermute | solution.py:27
  21.4 0.0 collective-permute-start.4
  21.4 0.0 collective-permute-done.p1
  21.4 0.5 collective-permute-start.6
  22.0 8.7 %collective-permute-done.1.p2 = bf16[64,1408]{1,0:T(8,128)(2,1)S(1)} collective-permute-done((bf16[64,1408]{1,0:T(8,128)(2,1)}, bf16[64,1408]{1,0:T(8,128)(2,1)S(1)}, u32[]{:S(2)}, u32[]{:S(2)}) %collective-permute-start.1) | collective-permute-done | bytes 180256 | tf_op jit(solution)/shard_map/sums0/ppermute | solution.py:27
  30.7 0.0 collective-permute-start.2
  30.7 0.0 collective-permute-done.7.rest_6_.rest_8_
  30.7 0.0 collective-permute-start.9
  30.7 0.0 collective-permute-done.8.rest_7_.rest_9_
  30.7 0.5 collective-permute-start.10
  31.2 0.3 multiply_sine_fusion
  31.5 0.1 pad_maximum_fusion.1
  31.6 4.8 %collective-permute-done.2.p3 = bf16[64,1408]{1,0:T(8,128)(2,1)S(1)} collective-permute-done((bf16[64,1408]{1,0:T(8,128)(2,1)}, bf16[64,1408]{1,0:T(8,128)(2,1)S(1)}, u32[]{:S(2)}, u32[]{:S(2)}) %collective-permute-start.2) | collective-permute-done | bytes 180256 | tf_op jit(solution)/shard_map/sums0/ppermute | solution.py:27
  36.4 0.0 collective-permute-start.14
  36.4 0.0 collective-permute-done.4.rest_3_.rest_5_
  36.4 2.9 %collective-permute-start.15 = (bf16[64,1408]{1,0:T(8,128)(2,1)}, bf16[64,1408]{1,0:T(8,128)(2,1)S(1)}, u32[]{:S(2)}, u32[]{:S(2)}) collective-permute-start(bf16[64,1408]{1,0:T(8,128)(2,1)} %get-tuple-element.36), channel_id=1, source_target_pairs={{0,16},{8,24},{16,0},{24,8},{1,17},{9,25},{17,1},{25,9},{2,18},{10... | collective-permute-start | bytes 540680 | tf_op jit(solution)/shard_map/sums1/ppermute | solution.py:27
  39.3 0.0 collective-permute-done.6.rest_5_.rest_7_
  39.3 0.5 collective-permute-start.16
  39.7 0.0 collective-permute-done.9.rest_8_.rest_10_
  39.7 0.0 collective-permute-done.10.rest_9_.rest_11_
  39.8 0.0 copy-start.6
  39.8 0.9 copy-done.6
  40.7 9.7 %attend.2 = (bf16[64,1024]{1,0:T(8,128)(2,1)S(1)}, bf16[64,128]{1,0:T(8,128)(2,1)S(1)}, bf16[64,128]{1,0:T(8,128)(2,1)S(1)}) custom-call(s32[4]{0:T(128)S(1)} %copy-done.3, s32[4,128]{1,0:T(4,128)S(1)} %copy-done.4, bf16[64,1408]{1,0:T(8,128)(2,1)S(1)} %copy-done.6, bf16[64,1408]{1,0:T(8,128)(2,1)S(1)} %collective-permute-done.p1, ...), custom_call_target="tpu_custom_call" | custom-call | flops 4294967296 | bytes 6291456 | tf_op jit(solution)/shard_map/attend/pallas_call | solution.py:261
  50.4 1.6 %collective-permute-start.11 = (bf16[64,1024]{1,0:T(8,128)(2,1)S(1)}, bf16[64,1024]{1,0:T(8,128)(2,1)S(1)}, u32[]{:S(2)}, u32[]{:S(2)}) collective-permute-start(bf16[64,1024]{1,0:T(8,128)(2,1)S(1)} %get-tuple-element.33.a0.before), channel_id=1, source_target_pairs={{0,8},{8,16},{16,24},{24,0},{1,9},{9,17},{17,25},{25,1},{2,10},{10... | collective-permute-start | bytes 393224 | tf_op jit(solution)/shard_map/gather0/ppermute | solution.py:27
  52.0 1.4 %collective-permute-start.12 = (bf16[64,1024]{1,0:T(8,128)(2,1)S(1)}, bf16[64,1024]{1,0:T(8,128)(2,1)S(1)}, u32[]{:S(2)}, u32[]{:S(2)}) collective-permute-start(bf16[64,1024]{1,0:T(8,128)(2,1)S(1)} %get-tuple-element.33.a0.before), channel_id=1, source_target_pairs={{0,16},{8,24},{16,0},{24,8},{1,17},{9,25},{17,1},{25,9},{2,18},{10... | collective-permute-start | bytes 393224 | tf_op jit(solution)/shard_map/gather0/ppermute | solution.py:27
  53.4 0.0 collective-permute-done.14.p1
  53.4 2.5 %collective-permute-start.13 = (bf16[64,1024]{1,0:T(8,128)(2,1)S(1)}, bf16[64,1024]{1,0:T(8,128)(2,1)S(1)}, u32[]{:S(2)}, u32[]{:S(2)}) collective-permute-start(bf16[64,1024]{1,0:T(8,128)(2,1)S(1)} %get-tuple-element.33.a0.before), channel_id=1, source_target_pairs={{0,24},{8,0},{16,8},{24,16},{1,25},{9,1},{17,9},{25,17},{2,26},{10... | collective-permute-start | bytes 393224 | tf_op jit(solution)/shard_map/gather0/ppermute | solution.py:27
  55.9 0.0 copy-start
  56.0 9.7 %attend.3.before.a0 = bf16[64,1024]{1,0:T(8,128)(2,1)S(1)} custom-call(s32[4]{0:T(128)S(1)} %copy-done.3, s32[4,128]{1,0:T(4,128)S(1)} %copy-done.4, bf16[64,1408]{1,0:T(8,128)(2,1)S(1)} %copy-done.5, bf16[64,1408]{1,0:T(8,128)(2,1)S(1)} %collective-permute-done.14.p1, bf16[64,1408]{1,0:T(8,128)(2,1)S(1)} %collective-permute-done.15.p2, ...), custom_call_target="tpu_custom_call" | custom-call | flops 4294967296 | bytes 6291456 | tf_op jit(solution)/shard_map/attend/pallas_call | solution.py:261
  65.7 0.0 collective-permute-done.12.a2
  65.7 0.0 collective-permute-done.13.a3
  65.7 3.1 %project_out.2 = (f32[2,256,256]{2,1,0:T(8,128)S(1)}, bf16[2,256,256]{2,1,0:T(8,128)(2,1)S(1)}, bf16[2,256,256]{2,1,0:T(8,128)(2,1)S(1)}, bf16[2,256,256]{2,1,0:T(8,128)(2,1)S(1)}, f32[8,128]{1,0:T(8,128)S(1)}) custom-call(s32[4]{0:T(128)S(1)} %copy-done.3, bf16[64,1024]{1,0:T(8,128)(2,1)S(1)} %get-tuple-element.33.a0.before, ...), custom_call_target="tpu_custom_call" | custom-call | flops 1073741824 | bytes 6291456 | tf_op jit(solution)/shard_map/project_out/pallas_call | solution.py:315
  68.8 1.8 %collective-permute-start.17 = (bf16[2,256,256]{2,1,0:T(8,128)(2,1)S(1)}, bf16[2,256,256]{2,1,0:T(8,128)(2,1)S(1)}, u32[]{:S(2)}, u32[]{:S(2)}) collective-permute-start(bf16[2,256,256]{2,1,0:T(8,128)(2,1)S(1)} %get-tuple-element.41), channel_id=1, source_target_pairs={{0,2},{1,3},{2,4},{3,5},{4,6},{5,7},{6,0},{7,1},{8,10},{9,11},{10,... | collective-permute-start | bytes 786440 | tf_op jit(solution)/shard_map/x0/ppermute | solution.py:32
  70.6 0.0 collective-permute-start.21
  70.6 1.7 %collective-permute-start.22 = (bf16[64,1024]{1,0:T(8,128)(2,1)S(1)}, bf16[64,1024]{1,0:T(8,128)(2,1)S(1)}, u32[]{:S(2)}, u32[]{:S(2)}) collective-permute-start(bf16[64,1024]{1,0:T(8,128)(2,1)S(1)} %attend.3.before.a0), channel_id=1, source_target_pairs={{0,16},{8,24},{16,0},{24,8},{1,17},{9,25},{17,1},{25,9},{2,18},{10... | collective-permute-start | bytes 393224 | tf_op jit(solution)/shard_map/gather1/ppermute | solution.py:27
  72.3 1.7 %collective-permute-start.23 = (bf16[64,1024]{1,0:T(8,128)(2,1)S(1)}, bf16[64,1024]{1,0:T(8,128)(2,1)S(1)}, u32[]{:S(2)}, u32[]{:S(2)}) collective-permute-start(bf16[64,1024]{1,0:T(8,128)(2,1)S(1)} %attend.3.before.a0), channel_id=1, source_target_pairs={{0,24},{8,0},{16,8},{24,16},{1,25},{9,1},{17,9},{25,17},{2,26},{10... | collective-permute-start | bytes 393224 | tf_op jit(solution)/shard_map/gather1/ppermute | solution.py:27
  74.0 1.1 %collective-permute-start.18 = (bf16[2,256,256]{2,1,0:T(8,128)(2,1)S(1)}, bf16[2,256,256]{2,1,0:T(8,128)(2,1)S(1)}, u32[]{:S(2)}, u32[]{:S(2)}) collective-permute-start(bf16[2,256,256]{2,1,0:T(8,128)(2,1)S(1)} %get-tuple-element.42), channel_id=1, source_target_pairs={{0,4},{1,5},{2,6},{3,7},{4,0},{5,1},{6,2},{7,3},{8,12},{9,13},{10,... | collective-permute-start | bytes 786440 | tf_op jit(solution)/shard_map/x0/ppermute | solution.py:32
  75.1 3.1 %collective-permute-done.21.a1 = bf16[64,1024]{1,0:T(8,128)(2,1)S(1)} collective-permute-done((bf16[64,1024]{1,0:T(8,128)(2,1)S(1)}, bf16[64,1024]{1,0:T(8,128)(2,1)S(1)}, u32[]{:S(2)}, u32[]{:S(2)}) %collective-permute-start.21) | collective-permute-done | bytes 131104 | tf_op jit(solution)/shard_map/gather1/ppermute | solution.py:27
  78.2 0.5 collective-permute-start.19
  78.7 0.4 collective-permute-done.23.a3
  79.1 3.2 %project_out.3 = (f32[2,256,256]{2,1,0:T(8,128)S(1)}, bf16[2,256,256]{2,1,0:T(8,128)(2,1)S(1)}, bf16[2,256,256]{2,1,0:T(8,128)(2,1)S(1)}, bf16[2,256,256]{2,1,0:T(8,128)(2,1)S(1)}, f32[8,128]{1,0:T(8,128)}) custom-call(s32[4]{0:T(128)S(1)} %copy-done.3, bf16[64,1024]{1,0:T(8,128)(2,1)S(1)} %attend.3.before.a0, ...), custom_call_target="tpu_custom_call" | custom-call | flops 1073741824 | bytes 6291456 | tf_op jit(solution)/shard_map/project_out/pallas_call | solution.py:315
  82.3 1.3 %collective-permute-start.24 = (bf16[2,256,256]{2,1,0:T(8,128)(2,1)S(1)}, bf16[2,256,256]{2,1,0:T(8,128)(2,1)S(1)}, u32[]{:S(2)}, u32[]{:S(2)}) collective-permute-start(bf16[2,256,256]{2,1,0:T(8,128)(2,1)S(1)} %get-tuple-element.48), channel_id=1, source_target_pairs={{0,2},{1,3},{2,4},{3,5},{4,6},{5,7},{6,0},{7,1},{8,10},{9,11},{10,... | collective-permute-start | bytes 786440 | tf_op jit(solution)/shard_map/x1/ppermute | solution.py:32
  83.6 2.2 %collective-permute-start.25 = (bf16[2,256,256]{2,1,0:T(8,128)(2,1)S(1)}, bf16[2,256,256]{2,1,0:T(8,128)(2,1)S(1)}, u32[]{:S(2)}, u32[]{:S(2)}) collective-permute-start(bf16[2,256,256]{2,1,0:T(8,128)(2,1)S(1)} %get-tuple-element.49), channel_id=1, source_target_pairs={{0,4},{1,5},{2,6},{3,7},{4,0},{5,1},{6,2},{7,3},{8,12},{9,13},{10,... | collective-permute-start | bytes 786440 | tf_op jit(solution)/shard_map/x1/ppermute | solution.py:32
  85.9 0.0 collective-permute-done.17.refs_1_
  85.9 1.0 collective-permute-start.26
  86.8 4.4 %collective-permute-done.19.refs_3_ = bf16[2,256,256]{2,1,0:T(8,128)(2,1)S(1)} collective-permute-done((bf16[2,256,256]{2,1,0:T(8,128)(2,1)S(1)}, bf16[2,256,256]{2,1,0:T(8,128)(2,1)S(1)}, u32[]{:S(2)}, u32[]{:S(2)}) %collective-permute-start.19) | collective-permute-done | bytes 262176 | tf_op jit(solution)/shard_map/x0/ppermute | solution.py:32
  91.2 0.7 reduce_pieces.2
  91.9 6.4 %collective-permute-start.20 = (bf16[256,256]{1,0:T(8,128)(2,1)S(1)}, bf16[256,256]{1,0:T(8,128)(2,1)S(1)}, u32[]{:S(2)}, u32[]{:S(2)}) collective-permute-start(bf16[256,256]{1,0:T(8,128)(2,1)S(1)} %get-tuple-element.45.before), channel_id=1, source_target_pairs={{0,1},{1,0},{2,3},{3,2},{4,5},{5,4},{6,7},{7,6},{8,9},{9,8},{10,11... | collective-permute-start | bytes 393224 | tf_op jit(solution)/shard_map/z0/ppermute | solution.py:38
  98.2 0.7 reduce_pieces.3
  98.9 4.0 %collective-permute-start.27 = (bf16[256,256]{1,0:T(8,128)(2,1)S(1)}, bf16[256,256]{1,0:T(8,128)(2,1)S(1)}, u32[]{:S(2)}, u32[]{:S(2)}) collective-permute-start(bf16[256,256]{1,0:T(8,128)(2,1)S(1)} %get-tuple-element.52), channel_id=1, source_target_pairs={{0,1},{1,0},{2,3},{3,2},{4,5},{5,4},{6,7},{7,6},{8,9},{9,8},{10,11... | collective-permute-start | bytes 393224 | tf_op jit(solution)/shard_map/z1/ppermute | solution.py:38
  102.9 1.5 %collective-permute-done.20 = bf16[256,256]{1,0:T(8,128)(2,1)S(1)} collective-permute-done((bf16[256,256]{1,0:T(8,128)(2,1)S(1)}, bf16[256,256]{1,0:T(8,128)(2,1)S(1)}, u32[]{:S(2)}, u32[]{:S(2)}) %collective-permute-start.20) | collective-permute-done | bytes 131104 | tf_op jit(solution)/shard_map/z0/ppermute | solution.py:38
  104.5 4.8 %collective-permute-done.27.arrived = bf16[256,256]{1,0:T(8,128)(2,1)S(1)} collective-permute-done((bf16[256,256]{1,0:T(8,128)(2,1)S(1)}, bf16[256,256]{1,0:T(8,128)(2,1)S(1)}, u32[]{:S(2)}, u32[]{:S(2)}) %collective-permute-start.27) | collective-permute-done | bytes 131104 | tf_op jit(solution)/shard_map/z1/ppermute | solution.py:38
  109.3 0.7 finish.1
  (24 shorter events, 0.1 us)
Async XLA Ops:
  1.1 15.0 %collective-permute-start.3 = (bf16[2,1024,128]{2,1,0:T(8,128)(2,1)S(1)}, bf16[2,1024,128]{2,1,0:T(8,128)(2,1)S(1)}, u32[]{:S(2)}, u32[]{:S(2)}) collective-permute-start(bf16[2,1024,128]{2,1,0:T(8,128)(2,1)S(1)} %pad_maximum_fusion), channel_id=1, source_target_pairs={{0,8},{8,16},{16,24},{24,0},{1,9},{9,17},{17,25},{25,1},{2,10},{10... | collective-permute-start | bytes 1572872 | tf_op jit(solution)/shard_map/cache/ppermute | solution.py:27
  2.8 14.9 %collective-permute-start.5 = (bf16[2,1024,128]{2,1,0:T(8,128)(2,1)S(1)}, bf16[2,1024,128]{2,1,0:T(8,128)(2,1)S(1)}, u32[]{:S(2)}, u32[]{:S(2)}) collective-permute-start(bf16[2,1024,128]{2,1,0:T(8,128)(2,1)S(1)} %pad_maximum_fusion), channel_id=1, source_target_pairs={{0,24},{8,0},{16,8},{24,16},{1,25},{9,1},{17,9},{25,17},{2,26},{10... | collective-permute-start | bytes 1572872 | tf_op jit(solution)/shard_map/cache/ppermute | solution.py:27
  5.1 34.7 %copy-start.1 = (bf16[2048,128]{1,0:T(8,128)(2,1)S(1)}, bf16[2048,128]{1,0:T(8,128)(2,1)}, u32[]{:S(2)}) copy-start(bf16[2048,128]{1,0:T(8,128)(2,1)} %rest_2_.1) | copy-start | bytes 1572868
  5.1 34.7 %copy-start.2 = (bf16[2048,128]{1,0:T(8,128)(2,1)S(1)}, bf16[2048,128]{1,0:T(8,128)(2,1)}, u32[]{:S(2)}) copy-start(bf16[2048,128]{1,0:T(8,128)(2,1)} %rest_3_.1) | copy-start | bytes 1572868
  5.1 34.7 %copy-start.3 = (s32[4]{0:T(128)S(1)}, s32[4]{0:T(128)}, u32[]{:S(2)}) copy-start(s32[4]{0:T(128)} %pad_add_fusion.place) | copy-start | bytes 52
  5.1 34.7 %copy-start.4 = (s32[4,128]{1,0:T(4,128)S(1)}, s32[4,128]{1,0:T(4,128)}, u32[]{:S(2)}) copy-start(s32[4,128]{1,0:T(4,128)} %mask.3) | copy-start | bytes 6148
  12.6 8.8 %collective-permute-start = (bf16[64,1408]{1,0:T(8,128)(2,1)}, bf16[64,1408]{1,0:T(8,128)(2,1)S(1)}, u32[]{:S(2)}, u32[]{:S(2)}) collective-permute-start(bf16[64,1408]{1,0:T(8,128)(2,1)} %get-tuple-element.30), channel_id=1, source_target_pairs={{0,8},{8,16},{16,24},{24,0},{1,9},{9,17},{17,25},{25,1},{2,10},{10... | collective-permute-start | bytes 540680 | tf_op jit(solution)/shard_map/sums0/ppermute | solution.py:27
  16.2 14.5 %collective-permute-start.7 = (bf16[1024,128]{1,0:T(8,128)(2,1)S(1)}, bf16[1024,128]{1,0:T(8,128)(2,1)S(1)}, u32[]{:S(2)}, u32[]{:S(2)}) collective-permute-start(bf16[1024,128]{1,0:T(8,128)(2,1)S(1)} %slice_bitcast_fusion.1), channel_id=1, source_target_pairs={{0,8},{8,16},{16,24},{24,0},{1,9},{9,17},{17,25},{25,1},{2,10},{10... | collective-permute-start | bytes 786440 | tf_op jit(solution)/shard_map/forward/ppermute | solution.py:27
  17.7 13.0 %collective-permute-start.8 = (bf16[1024,128]{1,0:T(8,128)(2,1)S(1)}, bf16[1024,128]{1,0:T(8,128)(2,1)S(1)}, u32[]{:S(2)}, u32[]{:S(2)}) collective-permute-start(bf16[1024,128]{1,0:T(8,128)(2,1)S(1)} %slice_bitcast_fusion), channel_id=1, source_target_pairs={{0,24},{8,0},{16,8},{24,16},{1,25},{9,1},{17,9},{25,17},{2,26},{10... | collective-permute-start | bytes 786440 | tf_op jit(solution)/shard_map/forward/ppermute | solution.py:27
  19.6 11.1 %collective-permute-start.1 = (bf16[64,1408]{1,0:T(8,128)(2,1)}, bf16[64,1408]{1,0:T(8,128)(2,1)S(1)}, u32[]{:S(2)}, u32[]{:S(2)}) collective-permute-start(bf16[64,1408]{1,0:T(8,128)(2,1)} %get-tuple-element.31), channel_id=1, source_target_pairs={{0,16},{8,24},{16,0},{24,8},{1,17},{9,25},{17,1},{25,9},{2,18},{10... | collective-permute-start | bytes 540680 | tf_op jit(solution)/shard_map/sums0/ppermute | solution.py:27
  21.4 14.9 %collective-permute-start.4 = (bf16[2,1024,128]{2,1,0:T(8,128)(2,1)S(1)}, bf16[2,1024,128]{2,1,0:T(8,128)(2,1)S(1)}, u32[]{:S(2)}, u32[]{:S(2)}) collective-permute-start(bf16[2,1024,128]{2,1,0:T(8,128)(2,1)S(1)} %collective-permute-done.3.rest_2_.rest_4_), channel_id=1, source_target_pairs={{0,32},{32,0},{64,96},{96,64},{128,160},{160,128},{192,224},{224,1... | collective-permute-start | bytes 1572872 | tf_op jit(solution)/shard_map/swap/ppermute | solution.py:42
  21.4 17.8 %collective-permute-start.6 = (bf16[2,1024,128]{2,1,0:T(8,128)(2,1)S(1)}, bf16[2,1024,128]{2,1,0:T(8,128)(2,1)S(1)}, u32[]{:S(2)}, u32[]{:S(2)}) collective-permute-start(bf16[2,1024,128]{2,1,0:T(8,128)(2,1)S(1)} %collective-permute-done.5.rest_4_.rest_6_), channel_id=1, source_target_pairs={{0,32},{32,0},{64,96},{96,64},{128,160},{160,128},{192,224},{224,1... | collective-permute-start | bytes 1572872 | tf_op jit(solution)/shard_map/swap/ppermute | solution.py:42
  30.7 5.7 %collective-permute-start.2 = (bf16[64,1408]{1,0:T(8,128)(2,1)}, bf16[64,1408]{1,0:T(8,128)(2,1)S(1)}, u32[]{:S(2)}, u32[]{:S(2)}) collective-permute-start(bf16[64,1408]{1,0:T(8,128)(2,1)} %get-tuple-element.32), channel_id=1, source_target_pairs={{0,24},{8,0},{16,8},{24,16},{1,25},{9,1},{17,9},{25,17},{2,26},{10... | collective-permute-start | bytes 540680 | tf_op jit(solution)/shard_map/sums0/ppermute | solution.py:27
  30.7 9.1 %collective-permute-start.9 = (bf16[1024,128]{1,0:T(8,128)(2,1)S(1)}, bf16[1024,128]{1,0:T(8,128)(2,1)S(1)}, u32[]{:S(2)}, u32[]{:S(2)}) collective-permute-start(bf16[1024,128]{1,0:T(8,128)(2,1)S(1)} %collective-permute-done.7.rest_6_.rest_8_), channel_id=1, source_target_pairs={{0,32},{32,0},{64,96},{96,64},{128,160},{160,128},{192,224},{224,1... | collective-permute-start | bytes 786440 | tf_op jit(solution)/shard_map/swap/ppermute | solution.py:42
  30.7 9.1 %collective-permute-start.10 = (bf16[1024,128]{1,0:T(8,128)(2,1)S(1)}, bf16[1024,128]{1,0:T(8,128)(2,1)S(1)}, u32[]{:S(2)}, u32[]{:S(2)}) collective-permute-start(bf16[1024,128]{1,0:T(8,128)(2,1)S(1)} %collective-permute-done.8.rest_7_.rest_9_), channel_id=1, source_target_pairs={{0,32},{32,0},{64,96},{96,64},{128,160},{160,128},{192,224},{224,1... | collective-permute-start | bytes 786440 | tf_op jit(solution)/shard_map/swap/ppermute | solution.py:42
  36.4 17.0 %collective-permute-start.14 = (bf16[64,1408]{1,0:T(8,128)(2,1)}, bf16[64,1408]{1,0:T(8,128)(2,1)S(1)}, u32[]{:S(2)}, u32[]{:S(2)}) collective-permute-start(bf16[64,1408]{1,0:T(8,128)(2,1)} %get-tuple-element.35), channel_id=1, source_target_pairs={{0,8},{8,16},{16,24},{24,0},{1,9},{9,17},{17,25},{25,1},{2,10},{10... | collective-permute-start | bytes 540680 | tf_op jit(solution)/shard_map/sums1/ppermute | solution.py:27
  36.4 19.6 %collective-permute-start.15 = (bf16[64,1408]{1,0:T(8,128)(2,1)}, bf16[64,1408]{1,0:T(8,128)(2,1)S(1)}, u32[]{:S(2)}, u32[]{:S(2)}) collective-permute-start(bf16[64,1408]{1,0:T(8,128)(2,1)} %get-tuple-element.36), channel_id=1, source_target_pairs={{0,16},{8,24},{16,0},{24,8},{1,17},{9,25},{17,1},{25,9},{2,18},{10... | collective-permute-start | bytes 540680 | tf_op jit(solution)/shard_map/sums1/ppermute | solution.py:27
  39.3 16.7 %collective-permute-start.16 = (bf16[64,1408]{1,0:T(8,128)(2,1)}, bf16[64,1408]{1,0:T(8,128)(2,1)S(1)}, u32[]{:S(2)}, u32[]{:S(2)}) collective-permute-start(bf16[64,1408]{1,0:T(8,128)(2,1)} %get-tuple-element.37), channel_id=1, source_target_pairs={{0,24},{8,0},{16,8},{24,16},{1,25},{9,1},{17,9},{25,17},{2,26},{10... | collective-permute-start | bytes 540680 | tf_op jit(solution)/shard_map/sums1/ppermute | solution.py:27
  39.8 0.9 copy-start.6
  40.7 15.2 %copy-start.5 = (bf16[64,1408]{1,0:T(8,128)(2,1)S(1)}, bf16[64,1408]{1,0:T(8,128)(2,1)}, u32[]{:S(2)}) copy-start(bf16[64,1408]{1,0:T(8,128)(2,1)} %get-tuple-element.34.p0) | copy-start | bytes 540676
  50.4 15.3 %collective-permute-start.11 = (bf16[64,1024]{1,0:T(8,128)(2,1)S(1)}, bf16[64,1024]{1,0:T(8,128)(2,1)S(1)}, u32[]{:S(2)}, u32[]{:S(2)}) collective-permute-start(bf16[64,1024]{1,0:T(8,128)(2,1)S(1)} %get-tuple-element.33.a0.before), channel_id=1, source_target_pairs={{0,8},{8,16},{16,24},{24,0},{1,9},{9,17},{17,25},{25,1},{2,10},{10... | collective-permute-start | bytes 393224 | tf_op jit(solution)/shard_map/gather0/ppermute | solution.py:27
  52.0 13.7 %collective-permute-start.12 = (bf16[64,1024]{1,0:T(8,128)(2,1)S(1)}, bf16[64,1024]{1,0:T(8,128)(2,1)S(1)}, u32[]{:S(2)}, u32[]{:S(2)}) collective-permute-start(bf16[64,1024]{1,0:T(8,128)(2,1)S(1)} %get-tuple-element.33.a0.before), channel_id=1, source_target_pairs={{0,16},{8,24},{16,0},{24,8},{1,17},{9,25},{17,1},{25,9},{2,18},{10... | collective-permute-start | bytes 393224 | tf_op jit(solution)/shard_map/gather0/ppermute | solution.py:27
  53.4 12.3 %collective-permute-start.13 = (bf16[64,1024]{1,0:T(8,128)(2,1)S(1)}, bf16[64,1024]{1,0:T(8,128)(2,1)S(1)}, u32[]{:S(2)}, u32[]{:S(2)}) collective-permute-start(bf16[64,1024]{1,0:T(8,128)(2,1)S(1)} %get-tuple-element.33.a0.before), channel_id=1, source_target_pairs={{0,24},{8,0},{16,8},{24,16},{1,25},{9,1},{17,9},{25,17},{2,26},{10... | collective-permute-start | bytes 393224 | tf_op jit(solution)/shard_map/gather0/ppermute | solution.py:27
  55.9 9.8 %copy-start = (bf16[1024,2048]{1,0:T(8,128)(2,1)S(1)}, bf16[1024,2048]{1,0:T(8,128)(2,1)}, u32[]{:S(2)}) copy-start(bf16[1024,2048]{1,0:T(8,128)(2,1)} %w_out.3) | copy-start | bytes 12582916
  68.8 17.0 %collective-permute-start.17 = (bf16[2,256,256]{2,1,0:T(8,128)(2,1)S(1)}, bf16[2,256,256]{2,1,0:T(8,128)(2,1)S(1)}, u32[]{:S(2)}, u32[]{:S(2)}) collective-permute-start(bf16[2,256,256]{2,1,0:T(8,128)(2,1)S(1)} %get-tuple-element.41), channel_id=1, source_target_pairs={{0,2},{1,3},{2,4},{3,5},{4,6},{5,7},{6,0},{7,1},{8,10},{9,11},{10,... | collective-permute-start | bytes 786440 | tf_op jit(solution)/shard_map/x0/ppermute | solution.py:32
  70.6 7.6 %collective-permute-start.21 = (bf16[64,1024]{1,0:T(8,128)(2,1)S(1)}, bf16[64,1024]{1,0:T(8,128)(2,1)S(1)}, u32[]{:S(2)}, u32[]{:S(2)}) collective-permute-start(bf16[64,1024]{1,0:T(8,128)(2,1)S(1)} %attend.3.before.a0), channel_id=1, source_target_pairs={{0,8},{8,16},{16,24},{24,0},{1,9},{9,17},{17,25},{25,1},{2,10},{10... | collective-permute-start | bytes 393224 | tf_op jit(solution)/shard_map/gather1/ppermute | solution.py:27
  70.6 8.1 %collective-permute-start.22 = (bf16[64,1024]{1,0:T(8,128)(2,1)S(1)}, bf16[64,1024]{1,0:T(8,128)(2,1)S(1)}, u32[]{:S(2)}, u32[]{:S(2)}) collective-permute-start(bf16[64,1024]{1,0:T(8,128)(2,1)S(1)} %attend.3.before.a0), channel_id=1, source_target_pairs={{0,16},{8,24},{16,0},{24,8},{1,17},{9,25},{17,1},{25,9},{2,18},{10... | collective-permute-start | bytes 393224 | tf_op jit(solution)/shard_map/gather1/ppermute | solution.py:27
  72.3 6.8 %collective-permute-start.23 = (bf16[64,1024]{1,0:T(8,128)(2,1)S(1)}, bf16[64,1024]{1,0:T(8,128)(2,1)S(1)}, u32[]{:S(2)}, u32[]{:S(2)}) collective-permute-start(bf16[64,1024]{1,0:T(8,128)(2,1)S(1)} %attend.3.before.a0), channel_id=1, source_target_pairs={{0,24},{8,0},{16,8},{24,16},{1,25},{9,1},{17,9},{25,17},{2,26},{10... | collective-permute-start | bytes 393224 | tf_op jit(solution)/shard_map/gather1/ppermute | solution.py:27
  74.0 12.8 %collective-permute-start.18 = (bf16[2,256,256]{2,1,0:T(8,128)(2,1)S(1)}, bf16[2,256,256]{2,1,0:T(8,128)(2,1)S(1)}, u32[]{:S(2)}, u32[]{:S(2)}) collective-permute-start(bf16[2,256,256]{2,1,0:T(8,128)(2,1)S(1)} %get-tuple-element.42), channel_id=1, source_target_pairs={{0,4},{1,5},{2,6},{3,7},{4,0},{5,1},{6,2},{7,3},{8,12},{9,13},{10,... | collective-permute-start | bytes 786440 | tf_op jit(solution)/shard_map/x0/ppermute | solution.py:32
  78.2 13.0 %collective-permute-start.19 = (bf16[2,256,256]{2,1,0:T(8,128)(2,1)S(1)}, bf16[2,256,256]{2,1,0:T(8,128)(2,1)S(1)}, u32[]{:S(2)}, u32[]{:S(2)}) collective-permute-start(bf16[2,256,256]{2,1,0:T(8,128)(2,1)S(1)} %get-tuple-element.43), channel_id=1, source_target_pairs={{0,6},{1,7},{2,0},{3,1},{4,2},{5,3},{6,4},{7,5},{8,14},{9,15},{10,... | collective-permute-start | bytes 786440 | tf_op jit(solution)/shard_map/x0/ppermute | solution.py:32
  82.3 15.9 %collective-permute-start.24 = (bf16[2,256,256]{2,1,0:T(8,128)(2,1)S(1)}, bf16[2,256,256]{2,1,0:T(8,128)(2,1)S(1)}, u32[]{:S(2)}, u32[]{:S(2)}) collective-permute-start(bf16[2,256,256]{2,1,0:T(8,128)(2,1)S(1)} %get-tuple-element.48), channel_id=1, source_target_pairs={{0,2},{1,3},{2,4},{3,5},{4,6},{5,7},{6,0},{7,1},{8,10},{9,11},{10,... | collective-permute-start | bytes 786440 | tf_op jit(solution)/shard_map/x1/ppermute | solution.py:32
  83.6 14.6 %collective-permute-start.25 = (bf16[2,256,256]{2,1,0:T(8,128)(2,1)S(1)}, bf16[2,256,256]{2,1,0:T(8,128)(2,1)S(1)}, u32[]{:S(2)}, u32[]{:S(2)}) collective-permute-start(bf16[2,256,256]{2,1,0:T(8,128)(2,1)S(1)} %get-tuple-element.49), channel_id=1, source_target_pairs={{0,4},{1,5},{2,6},{3,7},{4,0},{5,1},{6,2},{7,3},{8,12},{9,13},{10,... | collective-permute-start | bytes 786440 | tf_op jit(solution)/shard_map/x1/ppermute | solution.py:32
  85.9 12.4 %collective-permute-start.26 = (bf16[2,256,256]{2,1,0:T(8,128)(2,1)S(1)}, bf16[2,256,256]{2,1,0:T(8,128)(2,1)S(1)}, u32[]{:S(2)}, u32[]{:S(2)}) collective-permute-start(bf16[2,256,256]{2,1,0:T(8,128)(2,1)S(1)} %get-tuple-element.50), channel_id=1, source_target_pairs={{0,6},{1,7},{2,0},{3,1},{4,2},{5,3},{6,4},{7,5},{8,14},{9,15},{10,... | collective-permute-start | bytes 786440 | tf_op jit(solution)/shard_map/x1/ppermute | solution.py:32
  91.9 12.6 %collective-permute-start.20 = (bf16[256,256]{1,0:T(8,128)(2,1)S(1)}, bf16[256,256]{1,0:T(8,128)(2,1)S(1)}, u32[]{:S(2)}, u32[]{:S(2)}) collective-permute-start(bf16[256,256]{1,0:T(8,128)(2,1)S(1)} %get-tuple-element.45.before), channel_id=1, source_target_pairs={{0,1},{1,0},{2,3},{3,2},{4,5},{5,4},{6,7},{7,6},{8,9},{9,8},{10,11... | collective-permute-start | bytes 393224 | tf_op jit(solution)/shard_map/z0/ppermute | solution.py:38
  98.9 10.4 %collective-permute-start.27 = (bf16[256,256]{1,0:T(8,128)(2,1)S(1)}, bf16[256,256]{1,0:T(8,128)(2,1)S(1)}, u32[]{:S(2)}, u32[]{:S(2)}) collective-permute-start(bf16[256,256]{1,0:T(8,128)(2,1)S(1)} %get-tuple-element.52), channel_id=1, source_target_pairs={{0,1},{1,0},{2,3},{3,2},{4,5},{5,4},{6,7},{7,6},{8,9},{9,8},{10,11... | collective-permute-start | bytes 393224 | tf_op jit(solution)/shard_map/z1/ppermute | solution.py:38
where the time goes:
time: 112 us; the launch traced here: 110 us
  starting transfers between devices  40.6 us (36%)
  Pallas kernels  35.3 us (32%)
  waiting for transfers between devices  30.8 us (28%)
  local copies, waits for them, and re-layouts  2.04 us (2%)
  other arithmetic  1.15 us (1%)
    ppermute x16, starting transfers between devices, section_shift(): return lax.ppermute(x, 'section', [(i, (i + by) % n) for i in range(n)])  21.2 us
    ppermute x16, waiting for transfers between devices, section_shift(): return lax.ppermute(x, 'section', [(i, (i + by) % n) for i in range(n)])  20 us
    pallas_call x2, Pallas kernels, attend(): pl.pallas_call(functools.partial(attention_kernel, half), in_specs=[smem,...  19.4 us
    ppermute x2, starting transfers between devices, z_swap(): lax.ppermute(x, 'tensor', [(i, i ^ 1) for i in range(lax.axis_size('tenso...  10.4 us
    ppermute x6, starting transfers between devices, x_shift(): lax.ppermute(x, 'tensor', [(i, (i // 2 + by) % n * 2 + i % 2) for i in ra...  7.91 us
    pallas_call x1, Pallas kernels, project(): pl.pallas_call(project_kernel, in_specs=[smem, anywhere, vmem, anywhere,...  7.5 us
    pallas_call x2, Pallas kernels, project_out(): pl.pallas_call(output_kernel, in_specs=[smem] + [vmem] * count + [pl.Bloc...  6.31 us
    ppermute x2, waiting for transfers between devices, z_swap(): lax.ppermute(x, 'tensor', [(i, i ^ 1) for i in range(lax.axis_size('tenso...  6.3 us
  transfers between devices with their start and end apart: 28, of which 8 were waited for; matrix products, arithmetic and copies ran while one was open for 1% of the time, Pallas kernels for 29%

commit v1 on v0

--- a/solution.py
+++ b/solution.py
@@ -19,6 +19,7 @@
 F32 = jnp.float32
 HALVES = 2
 TILE = 1024
+LOOPS = 2
 MIB = 1024 * 1024
 
 
@@ -217,30 +218,35 @@
     for copy in copies:
         copy.wait()
 
-    def score(t, buffer):
-        at = pl.ds(pl.multiple_of(t * tile, tile), tile)
-        s = lax.dot_general(q_aug, keys[at], dims, preferred_element_type=F32)
-        buffer[...] = s
-        return jnp.max(s, axis=-1, keepdims=True)
-
-    def weigh(t, buffer, m, m_new, acc):
-        at = pl.ds(pl.multiple_of(t * tile, tile), tile)
-        p = jnp.exp2(buffer[...] - m_new).astype(BF)
-        return acc * jnp.exp2(m - m_new) + jnp.dot(p, values[at], preferred_element_type=F32)
-
-    def pair(i, state):
-        m, top, acc = state
-        t = 2 * i
-        m_new = jnp.maximum(m, top)
-        top = score(t + 1, buf1)
-        acc = weigh(t, buf0, m, m_new, acc)
-        m = m_new
-        m_new = jnp.maximum(m, top)
-        top = score(lax.rem(t + 2, tiles), buf0)
-        acc = weigh(t + 1, buf1, m, m_new, acc)
-        return m_new, top, acc
-
-    m, _, acc = lax.fori_loop(0, tiles // 2, pair, (m, score(0, buf0), acc))
+    buffers = (buf0, buf1)
+    each = tiles // LOOPS
+
+    def at(t):
+        return pl.ds(pl.multiple_of(t * tile, tile), tile)
+
+    def sweep(i, state):
+        m, acc = state
+
+        def score(t):
+            s = lax.dot_general(
+                q_aug, keys[at(i * each + t)], dims, preferred_element_type=F32
+            )
+            buffers[t % 2][...] = s
+            return jnp.max(s, axis=-1, keepdims=True)
+
+        top = score(0)
+        for t in range(each):
+            m_new = jnp.maximum(m, top)
+            if t + 1 < each:
+                top = score(t + 1)
+            p = jnp.exp2(buffers[t % 2][...] - m_new).astype(BF)
+            acc = acc * jnp.exp2(m - m_new) + jnp.dot(
+                p, values[at(i * each + t)], preferred_element_type=F32
+            )
+            m = m_new
+        return m, acc
+
+    m, acc = lax.fori_loop(0, LOOPS, sweep, (m, acc))
     result = (acc[:, :HD] / acc[:, HD : HD + 1]).astype(BF)
     for h in range(heads):
         out[:, h * HD : (h + 1) * HD] = result[h * span : (h + 1) * span]
@@ -418,7 +424,7 @@
     for h in range(HALVES):
         with jax.named_scope(f"sums{h}"):
             parts.append(
-                [chunks[h]] + [section_shift(chunks[r * HALVES + h], r) for r in (1, 2, 3)]
+                [chunks[h]] + [section_shift(chunks[r * HALVES + h], r) for r in (2, 1, 3)]
             )
     before, attended, gathered = [], [], []
     for h in range(HALVES):
@@ -435,7 +441,7 @@
     for h in range(HALVES):
         *sums, turn = project_out(place, gathered[h], w_out, turn)
         with jax.named_scope(f"x{h}"):
-            pieces = [sums[0]] + [x_shift(sums[r], r) for r in (1, 2, 3)]
+            pieces = [sums[0]] + [x_shift(sums[r], r) for r in (2, 1, 3)]
         send, keep = reduce_pieces(place, send, pieces)
         with jax.named_scope(f"z{h}"):
             arrived = z_swap(send)

time: 112 us -> 108 us (0.964)
  waiting for transfers between devices: 30.8 us -> 28.4 us
  Pallas kernels: 35.3 us -> 33.1 us
  starting transfers between devices: 40.6 us -> 41.8 us
    pallas_call x2, Pallas kernels: 19.4 us -> 17.3 us  [attend(): pl.pallas_call(functools.partial(attention_kernel, half), in_specs=[smem,...]
    ppermute x16, starting transfers between devices: 21.2 us -> 23.4 us  [section_shift(): return lax.ppermute(x, 'section', [(i, (i + by) % n) for i in range(n)])]
    ppermute x16, waiting for transfers between devices: 20 us -> 18.4 us  [section_shift(): return lax.ppermute(x, 'section', [(i, (i + by) % n) for i in range(n)])]
    ppermute x6, starting transfers between devices: 7.91 us -> 6.58 us  [x_shift(): lax.ppermute(x, 'tensor', [(i, (i // 2 + by) % n * 2 + i % 2) for i in ra...]
    ppermute x2, waiting for transfers between devices: 6.3 us -> 5.16 us  [z_swap(): lax.ppermute(x, 'tensor', [(i, i ^ 1) for i in range(lax.axis_size('tenso...]
  transfers between devices with their start and end apart: 28 -> 28, of which waited for: 8 -> 7; matrix products, arithmetic and copies ran while one was open for 1% -> 1% of each run, Pallas kernels for 29% -> 27%
where the time goes in v1:
time: 108 us; the launch traced here: 107 us
  starting transfers between devices  41.8 us (39%)
  Pallas kernels  33.1 us (31%)
  waiting for transfers between devices  28.4 us (26%)
  local copies, waits for them, and re-layouts  2.04 us (2%)
  other arithmetic  1.15 us (1%)
    ppermute x16, starting transfers between devices, section_shift(): return lax.ppermute(x, 'section', [(i, (i + by) % n) for i in range(n)])  23.4 us
    ppermute x16, waiting for transfers between devices, section_shift(): return lax.ppermute(x, 'section', [(i, (i + by) % n) for i in range(n)])  18.4 us
    pallas_call x2, Pallas kernels, attend(): pl.pallas_call(functools.partial(attention_kernel, half), in_specs=[smem,...  17.3 us
    ppermute x2, starting transfers between devices, z_swap(): lax.ppermute(x, 'tensor', [(i, i ^ 1) for i in range(lax.axis_size('tenso...  10.9 us
    pallas_call x1, Pallas kernels, project(): pl.pallas_call(project_kernel, in_specs=[smem, anywhere, vmem, anywhere,...  7.5 us
    ppermute x6, starting transfers between devices, x_shift(): lax.ppermute(x, 'tensor', [(i, (i // 2 + by) % n * 2 + i % 2) for i in ra...  6.58 us
    pallas_call x2, Pallas kernels, project_out(): pl.pallas_call(output_kernel, in_specs=[smem] + [vmem] * count + [pl.Bloc...  6.31 us
    ppermute x2, waiting for transfers between devices, z_swap(): lax.ppermute(x, 'tensor', [(i, i ^ 1) for i in range(lax.axis_size('tenso...  5.16 us
  transfers between devices with their start and end apart: 28, of which 7 were waited for; matrix products, arithmetic and copies ran while one was open for 1% of the time, Pallas kernels for 27%

profile of v1, /device:TPU:34, one launch (start us, length us, event | category | flops | bytes accessed | tf_op | source)
XLA Modules:
  0.0 106.8 jit_solution(17893052449187307051)
XLA Ops:
  0.0 1.1 dynamic-slice_bitcast_fusion
  1.1 0.1 pad_maximum_fusion
  1.1 1.7 %collective-permute-start.3 = (bf16[2,1024,128]{2,1,0:T(8,128)(2,1)S(1)}, bf16[2,1024,128]{2,1,0:T(8,128)(2,1)S(1)}, u32[]{:S(2)}, u32[]{:S(2)}) collective-permute-start(bf16[2,1024,128]{2,1,0:T(8,128)(2,1)S(1)} %pad_maximum_fusion), channel_id=1, source_target_pairs={{0,8},{8,16},{16,24},{24,0},{1,9},{9,17},{17,25},{25,1},{2,10},{10... | collective-permute-start | bytes 1572872 | tf_op jit(solution)/shard_map/cache/ppermute | solution.py:28
  2.8 1.7 %collective-permute-start.5 = (bf16[2,1024,128]{2,1,0:T(8,128)(2,1)S(1)}, bf16[2,1024,128]{2,1,0:T(8,128)(2,1)S(1)}, u32[]{:S(2)}, u32[]{:S(2)}) collective-permute-start(bf16[2,1024,128]{2,1,0:T(8,128)(2,1)S(1)} %pad_maximum_fusion), channel_id=1, source_target_pairs={{0,24},{8,0},{16,8},{24,16},{1,25},{9,1},{17,9},{25,17},{2,26},{10... | collective-permute-start | bytes 1572872 | tf_op jit(solution)/shard_map/cache/ppermute | solution.py:28
  4.4 0.7 pad_add_fusion.place
  5.1 7.5 %project.1 = (bf16[64,1408]{1,0:T(8,128)(2,1)}, bf16[64,1408]{1,0:T(8,128)(2,1)}, bf16[64,1408]{1,0:T(8,128)(2,1)}, bf16[64,1408]{1,0:T(8,128)(2,1)}, bf16[64,14...) custom-call(s32[4]{0:T(128)} %pad_add_fusion.place, ...), custom_call_target="tpu_custom_call" | custom-call | flops 2684354560 | bytes 9437184 | tf_op jit(solution)/shard_map/project/pallas_call | solution.py:106
  12.6 2.1 %collective-permute-start = (bf16[64,1408]{1,0:T(8,128)(2,1)}, bf16[64,1408]{1,0:T(8,128)(2,1)S(1)}, u32[]{:S(2)}, u32[]{:S(2)}) collective-permute-start(bf16[64,1408]{1,0:T(8,128)(2,1)} %get-tuple-element.30), channel_id=1, source_target_pairs={{0,16},{8,24},{16,0},{24,8},{1,17},{9,25},{17,1},{25,9},{2,18},{10... | collective-permute-start | bytes 540680 | tf_op jit(solution)/shard_map/sums0/ppermute | solution.py:28
  14.7 1.5 %collective-permute-done.3.rest_2_.rest_4_ = bf16[2,1024,128]{2,1,0:T(8,128)(2,1)S(1)} collective-permute-done((bf16[2,1024,128]{2,1,0:T(8,128)(2,1)S(1)}, bf16[2,1024,128]{2,1,0:T(8,128)(2,1)S(1)}, u32[]{:S(2)}, u32[]{:S(2)}) %collective-permute-start.3) | collective-permute-done | bytes 524320 | tf_op jit(solution)/shard_map/cache/ppermute | solution.py:28
  16.2 0.4 collective-permute-start.7
  16.5 2.0 %collective-permute-done.5.rest_4_.rest_6_ = bf16[2,1024,128]{2,1,0:T(8,128)(2,1)S(1)} collective-permute-done((bf16[2,1024,128]{2,1,0:T(8,128)(2,1)S(1)}, bf16[2,1024,128]{2,1,0:T(8,128)(2,1)S(1)}, u32[]{:S(2)}, u32[]{:S(2)}) %collective-permute-start.5) | collective-permute-done | bytes 524320 | tf_op jit(solution)/shard_map/cache/ppermute | solution.py:28
  18.5 4.0 %collective-permute-start.8 = (bf16[1024,128]{1,0:T(8,128)(2,1)S(1)}, bf16[1024,128]{1,0:T(8,128)(2,1)S(1)}, u32[]{:S(2)}, u32[]{:S(2)}) collective-permute-start(bf16[1024,128]{1,0:T(8,128)(2,1)S(1)} %slice_bitcast_fusion), channel_id=1, source_target_pairs={{0,24},{8,0},{16,8},{24,16},{1,25},{9,1},{17,9},{25,17},{2,26},{10... | collective-permute-start | bytes 786440 | tf_op jit(solution)/shard_map/forward/ppermute | solution.py:28
  22.5 0.0 collective-permute-start.1
  22.5 0.5 collective-permute-start.6
  23.0 7.6 %collective-permute-done.1.p2 = bf16[64,1408]{1,0:T(8,128)(2,1)S(1)} collective-permute-done((bf16[64,1408]{1,0:T(8,128)(2,1)}, bf16[64,1408]{1,0:T(8,128)(2,1)S(1)}, u32[]{:S(2)}, u32[]{:S(2)}) %collective-permute-start.1) | collective-permute-done | bytes 180256 | tf_op jit(solution)/shard_map/sums0/ppermute | solution.py:28
  30.7 0.6 collective-permute-start.2
  31.2 0.0 collective-permute-start.9
  31.2 0.0 collective-permute-done.8.rest_7_.rest_9_
  31.2 0.5 collective-permute-start.10
  31.7 0.3 multiply_sine_fusion
  32.1 0.1 pad_maximum_fusion.1
  32.2 4.5 %collective-permute-done.2.p3 = bf16[64,1408]{1,0:T(8,128)(2,1)S(1)} collective-permute-done((bf16[64,1408]{1,0:T(8,128)(2,1)}, bf16[64,1408]{1,0:T(8,128)(2,1)S(1)}, u32[]{:S(2)}, u32[]{:S(2)}) %collective-permute-start.2) | collective-permute-done | bytes 180256 | tf_op jit(solution)/shard_map/sums0/ppermute | solution.py:28
  36.7 0.9 collective-permute-start.14
  37.6 1.6 %collective-permute-start.15 = (bf16[64,1408]{1,0:T(8,128)(2,1)}, bf16[64,1408]{1,0:T(8,128)(2,1)S(1)}, u32[]{:S(2)}, u32[]{:S(2)}) collective-permute-start(bf16[64,1408]{1,0:T(8,128)(2,1)} %get-tuple-element.36), channel_id=1, source_target_pairs={{0,8},{8,16},{16,24},{24,0},{1,9},{9,17},{17,25},{25,1},{2,10},{10... | collective-permute-start | bytes 540680 | tf_op jit(solution)/shard_map/sums1/ppermute | solution.py:28
  39.3 0.0 collective-permute-done.6.rest_5_.rest_7_
  39.3 1.6 %collective-permute-start.16 = (bf16[64,1408]{1,0:T(8,128)(2,1)}, bf16[64,1408]{1,0:T(8,128)(2,1)S(1)}, u32[]{:S(2)}, u32[]{:S(2)}) collective-permute-start(bf16[64,1408]{1,0:T(8,128)(2,1)} %get-tuple-element.37), channel_id=1, source_target_pairs={{0,24},{8,0},{16,8},{24,16},{1,25},{9,1},{17,9},{25,17},{2,26},{10... | collective-permute-start | bytes 540680 | tf_op jit(solution)/shard_map/sums1/ppermute | solution.py:28
  40.9 0.0 collective-permute-done.9.rest_8_.rest_10_
  40.9 0.0 collective-permute-done.10.rest_9_.rest_11_
  40.9 0.0 copy-start.6
  40.9 0.9 copy-done.6
  41.8 8.6 %attend.2 = (bf16[64,1024]{1,0:T(8,128)(2,1)S(1)}, bf16[64,128]{1,0:T(8,128)(2,1)S(1)}, bf16[64,128]{1,0:T(8,128)(2,1)S(1)}) custom-call(s32[4]{0:T(128)S(1)} %copy-done.3, s32[4,128]{1,0:T(4,128)S(1)} %copy-done.4, bf16[64,1408]{1,0:T(8,128)(2,1)S(1)} %copy-done.6, bf16[64,1408]{1,0:T(8,128)(2,1)S(1)} %collective-permute-done.p1, ...), custom_call_target="tpu_custom_call" | custom-call | flops 4294967296 | bytes 6291456 | tf_op jit(solution)/shard_map/attend/pallas_call | solution.py:267
  50.5 0.5 collective-permute-start.11
  51.0 1.2 %collective-permute-start.12 = (bf16[64,1024]{1,0:T(8,128)(2,1)S(1)}, bf16[64,1024]{1,0:T(8,128)(2,1)S(1)}, u32[]{:S(2)}, u32[]{:S(2)}) collective-permute-start(bf16[64,1024]{1,0:T(8,128)(2,1)S(1)} %get-tuple-element.33.a0.before), channel_id=1, source_target_pairs={{0,16},{8,24},{16,0},{24,8},{1,17},{9,25},{17,1},{25,9},{2,18},{10... | collective-permute-start | bytes 393224 | tf_op jit(solution)/shard_map/gather0/ppermute | solution.py:28
  52.2 0.0 collective-permute-done.14.p1
  52.2 2.4 %collective-permute-start.13 = (bf16[64,1024]{1,0:T(8,128)(2,1)S(1)}, bf16[64,1024]{1,0:T(8,128)(2,1)S(1)}, u32[]{:S(2)}, u32[]{:S(2)}) collective-permute-start(bf16[64,1024]{1,0:T(8,128)(2,1)S(1)} %get-tuple-element.33.a0.before), channel_id=1, source_target_pairs={{0,24},{8,0},{16,8},{24,16},{1,25},{9,1},{17,9},{25,17},{2,26},{10... | collective-permute-start | bytes 393224 | tf_op jit(solution)/shard_map/gather0/ppermute | solution.py:28
  54.6 0.0 collective-permute-done.15.p2
  54.6 0.0 collective-permute-done.16.p3
  54.6 0.0 copy-start
  54.6 8.6 %attend.3.before.a0 = bf16[64,1024]{1,0:T(8,128)(2,1)S(1)} custom-call(s32[4]{0:T(128)S(1)} %copy-done.3, s32[4,128]{1,0:T(4,128)S(1)} %copy-done.4, bf16[64,1408]{1,0:T(8,128)(2,1)S(1)} %copy-done.5, bf16[64,1408]{1,0:T(8,128)(2,1)S(1)} %collective-permute-done.14.p1, bf16[64,1408]{1,0:T(8,128)(2,1)S(1)} %collective-permute-done.15.p2, ...), custom_call_target="tpu_custom_call" | custom-call | flops 4294967296 | bytes 6291456 | tf_op jit(solution)/shard_map/attend/pallas_call | solution.py:267
  63.2 0.0 collective-permute-done.11.a1
  63.2 0.0 collective-permute-done.12.a2
  63.3 3.1 %project_out.2 = (f32[2,256,256]{2,1,0:T(8,128)S(1)}, bf16[2,256,256]{2,1,0:T(8,128)(2,1)S(1)}, bf16[2,256,256]{2,1,0:T(8,128)(2,1)S(1)}, bf16[2,256,256]{2,1,0:T(8,128)(2,1)S(1)}, f32[8,128]{1,0:T(8,128)S(1)}) custom-call(s32[4]{0:T(128)S(1)} %copy-done.3, bf16[64,1024]{1,0:T(8,128)(2,1)S(1)} %get-tuple-element.33.a0.before, ...), custom_call_target="tpu_custom_call" | custom-call | flops 1073741824 | bytes 6291456 | tf_op jit(solution)/shard_map/project_out/pallas_call | solution.py:321
  66.4 2.2 %collective-permute-start.17 = (bf16[2,256,256]{2,1,0:T(8,128)(2,1)S(1)}, bf16[2,256,256]{2,1,0:T(8,128)(2,1)S(1)}, u32[]{:S(2)}, u32[]{:S(2)}) collective-permute-start(bf16[2,256,256]{2,1,0:T(8,128)(2,1)S(1)} %get-tuple-element.41), channel_id=1, source_target_pairs={{0,4},{1,5},{2,6},{3,7},{4,0},{5,1},{6,2},{7,3},{8,12},{9,13},{10,... | collective-permute-start | bytes 786440 | tf_op jit(solution)/shard_map/x0/ppermute | solution.py:33
  68.6 0.1 collective-permute-start.21
  68.7 2.1 %collective-permute-start.22 = (bf16[64,1024]{1,0:T(8,128)(2,1)S(1)}, bf16[64,1024]{1,0:T(8,128)(2,1)S(1)}, u32[]{:S(2)}, u32[]{:S(2)}) collective-permute-start(bf16[64,1024]{1,0:T(8,128)(2,1)S(1)} %attend.3.before.a0), channel_id=1, source_target_pairs={{0,16},{8,24},{16,0},{24,8},{1,17},{9,25},{17,1},{25,9},{2,18},{10... | collective-permute-start | bytes 393224 | tf_op jit(solution)/shard_map/gather1/ppermute | solution.py:28
  70.7 2.6 %collective-permute-start.23 = (bf16[64,1024]{1,0:T(8,128)(2,1)S(1)}, bf16[64,1024]{1,0:T(8,128)(2,1)S(1)}, u32[]{:S(2)}, u32[]{:S(2)}) collective-permute-start(bf16[64,1024]{1,0:T(8,128)(2,1)S(1)} %attend.3.before.a0), channel_id=1, source_target_pairs={{0,24},{8,0},{16,8},{24,16},{1,25},{9,1},{17,9},{25,17},{2,26},{10... | collective-permute-start | bytes 393224 | tf_op jit(solution)/shard_map/gather1/ppermute | solution.py:28
  73.4 2.8 %collective-permute-done.21.a1 = bf16[64,1024]{1,0:T(8,128)(2,1)S(1)} collective-permute-done((bf16[64,1024]{1,0:T(8,128)(2,1)S(1)}, bf16[64,1024]{1,0:T(8,128)(2,1)S(1)}, u32[]{:S(2)}, u32[]{:S(2)}) %collective-permute-start.21) | collective-permute-done | bytes 131104 | tf_op jit(solution)/shard_map/gather1/ppermute | solution.py:28
  76.2 1.4 %collective-permute-start.19 = (bf16[2,256,256]{2,1,0:T(8,128)(2,1)S(1)}, bf16[2,256,256]{2,1,0:T(8,128)(2,1)S(1)}, u32[]{:S(2)}, u32[]{:S(2)}) collective-permute-start(bf16[2,256,256]{2,1,0:T(8,128)(2,1)S(1)} %get-tuple-element.43), channel_id=1, source_target_pairs={{0,6},{1,7},{2,0},{3,1},{4,2},{5,3},{6,4},{7,5},{8,14},{9,15},{10,... | collective-permute-start | bytes 786440 | tf_op jit(solution)/shard_map/x0/ppermute | solution.py:33
  77.6 0.0 collective-permute-done.22.a2
  77.6 3.2 %project_out.3 = (f32[2,256,256]{2,1,0:T(8,128)S(1)}, bf16[2,256,256]{2,1,0:T(8,128)(2,1)S(1)}, bf16[2,256,256]{2,1,0:T(8,128)(2,1)S(1)}, bf16[2,256,256]{2,1,0:T(8,128)(2,1)S(1)}, f32[8,128]{1,0:T(8,128)}) custom-call(s32[4]{0:T(128)S(1)} %copy-done.3, bf16[64,1024]{1,0:T(8,128)(2,1)S(1)} %attend.3.before.a0, ...), custom_call_target="tpu_custom_call" | custom-call | flops 1073741824 | bytes 6291456 | tf_op jit(solution)/shard_map/project_out/pallas_call | solution.py:321
  80.8 0.9 collective-permute-start.24
  81.7 1.8 %collective-permute-start.25 = (bf16[2,256,256]{2,1,0:T(8,128)(2,1)S(1)}, bf16[2,256,256]{2,1,0:T(8,128)(2,1)S(1)}, u32[]{:S(2)}, u32[]{:S(2)}) collective-permute-start(bf16[2,256,256]{2,1,0:T(8,128)(2,1)S(1)} %get-tuple-element.49), channel_id=1, source_target_pairs={{0,2},{1,3},{2,4},{3,5},{4,6},{5,7},{6,0},{7,1},{8,10},{9,11},{10,... | collective-permute-start | bytes 786440 | tf_op jit(solution)/shard_map/x1/ppermute | solution.py:33
  83.5 0.0 collective-permute-done.17.refs_1_
  83.5 0.2 collective-permute-start.26
  83.8 0.0 collective-permute-done.18.refs_2_
  83.8 4.8 %collective-permute-done.19.refs_3_ = bf16[2,256,256]{2,1,0:T(8,128)(2,1)S(1)} collective-permute-done((bf16[2,256,256]{2,1,0:T(8,128)(2,1)S(1)}, bf16[2,256,256]{2,1,0:T(8,128)(2,1)S(1)}, u32[]{:S(2)}, u32[]{:S(2)}) %collective-permute-start.19) | collective-permute-done | bytes 262176 | tf_op jit(solution)/shard_map/x0/ppermute | solution.py:33
  88.6 0.7 reduce_pieces.2
  89.3 6.4 %collective-permute-start.20 = (bf16[256,256]{1,0:T(8,128)(2,1)S(1)}, bf16[256,256]{1,0:T(8,128)(2,1)S(1)}, u32[]{:S(2)}, u32[]{:S(2)}) collective-permute-start(bf16[256,256]{1,0:T(8,128)(2,1)S(1)} %get-tuple-element.45.before), channel_id=1, source_target_pairs={{0,1},{1,0},{2,3},{3,2},{4,5},{5,4},{6,7},{7,6},{8,9},{9,8},{10,11... | collective-permute-start | bytes 393224 | tf_op jit(solution)/shard_map/z0/ppermute | solution.py:39
  95.6 0.0 collective-permute-done.24.refs_1_
  95.6 0.0 collective-permute-done.25.refs_2_
  95.6 0.0 collective-permute-done.26.refs_3_
  95.7 0.7 reduce_pieces.3
  96.3 4.5 %collective-permute-start.27 = (bf16[256,256]{1,0:T(8,128)(2,1)S(1)}, bf16[256,256]{1,0:T(8,128)(2,1)S(1)}, u32[]{:S(2)}, u32[]{:S(2)}) collective-permute-start(bf16[256,256]{1,0:T(8,128)(2,1)S(1)} %get-tuple-element.52), channel_id=1, source_target_pairs={{0,1},{1,0},{2,3},{3,2},{4,5},{5,4},{6,7},{7,6},{8,9},{9,8},{10,11... | collective-permute-start | bytes 393224 | tf_op jit(solution)/shard_map/z1/ppermute | solution.py:39
  100.8 5.2 %collective-permute-done.27.arrived = bf16[256,256]{1,0:T(8,128)(2,1)S(1)} collective-permute-done((bf16[256,256]{1,0:T(8,128)(2,1)S(1)}, bf16[256,256]{1,0:T(8,128)(2,1)S(1)}, u32[]{:S(2)}, u32[]{:S(2)}) %collective-permute-start.27) | collective-permute-done | bytes 131104 | tf_op jit(solution)/shard_map/z1/ppermute | solution.py:39
  106.0 0.7 finish.1
  (24 shorter events, 0.1 us)
Async XLA Ops:
  1.1 15.0 %collective-permute-start.3 = (bf16[2,1024,128]{2,1,0:T(8,128)(2,1)S(1)}, bf16[2,1024,128]{2,1,0:T(8,128)(2,1)S(1)}, u32[]{:S(2)}, u32[]{:S(2)}) collective-permute-start(bf16[2,1024,128]{2,1,0:T(8,128)(2,1)S(1)} %pad_maximum_fusion), channel_id=1, source_target_pairs={{0,8},{8,16},{16,24},{24,0},{1,9},{9,17},{17,25},{25,1},{2,10},{10... | collective-permute-start | bytes 1572872 | tf_op jit(solution)/shard_map/cache/ppermute | solution.py:28
  2.8 15.7 %collective-permute-start.5 = (bf16[2,1024,128]{2,1,0:T(8,128)(2,1)S(1)}, bf16[2,1024,128]{2,1,0:T(8,128)(2,1)S(1)}, u32[]{:S(2)}, u32[]{:S(2)}) collective-permute-start(bf16[2,1024,128]{2,1,0:T(8,128)(2,1)S(1)} %pad_maximum_fusion), channel_id=1, source_target_pairs={{0,24},{8,0},{16,8},{24,16},{1,25},{9,1},{17,9},{25,17},{2,26},{10... | collective-permute-start | bytes 1572872 | tf_op jit(solution)/shard_map/cache/ppermute | solution.py:28
  5.1 35.8 %copy-start.1 = (bf16[2048,128]{1,0:T(8,128)(2,1)S(1)}, bf16[2048,128]{1,0:T(8,128)(2,1)}, u32[]{:S(2)}) copy-start(bf16[2048,128]{1,0:T(8,128)(2,1)} %rest_2_.1) | copy-start | bytes 1572868
  5.1 35.8 %copy-start.2 = (bf16[2048,128]{1,0:T(8,128)(2,1)S(1)}, bf16[2048,128]{1,0:T(8,128)(2,1)}, u32[]{:S(2)}) copy-start(bf16[2048,128]{1,0:T(8,128)(2,1)} %rest_3_.1) | copy-start | bytes 1572868
  5.1 35.8 %copy-start.3 = (s32[4]{0:T(128)S(1)}, s32[4]{0:T(128)}, u32[]{:S(2)}) copy-start(s32[4]{0:T(128)} %pad_add_fusion.place) | copy-start | bytes 52
  5.1 35.8 %copy-start.4 = (s32[4,128]{1,0:T(4,128)S(1)}, s32[4,128]{1,0:T(4,128)}, u32[]{:S(2)}) copy-start(s32[4,128]{1,0:T(4,128)} %mask.3) | copy-start | bytes 6148
  12.6 9.9 %collective-permute-start = (bf16[64,1408]{1,0:T(8,128)(2,1)}, bf16[64,1408]{1,0:T(8,128)(2,1)S(1)}, u32[]{:S(2)}, u32[]{:S(2)}) collective-permute-start(bf16[64,1408]{1,0:T(8,128)(2,1)} %get-tuple-element.30), channel_id=1, source_target_pairs={{0,16},{8,24},{16,0},{24,8},{1,17},{9,25},{17,1},{25,9},{2,18},{10... | collective-permute-start | bytes 540680 | tf_op jit(solution)/shard_map/sums0/ppermute | solution.py:28
  16.2 15.1 %collective-permute-start.7 = (bf16[1024,128]{1,0:T(8,128)(2,1)S(1)}, bf16[1024,128]{1,0:T(8,128)(2,1)S(1)}, u32[]{:S(2)}, u32[]{:S(2)}) collective-permute-start(bf16[1024,128]{1,0:T(8,128)(2,1)S(1)} %slice_bitcast_fusion.1), channel_id=1, source_target_pairs={{0,8},{8,16},{16,24},{24,0},{1,9},{9,17},{17,25},{25,1},{2,10},{10... | collective-permute-start | bytes 786440 | tf_op jit(solution)/shard_map/forward/ppermute | solution.py:28
  18.5 12.7 %collective-permute-start.8 = (bf16[1024,128]{1,0:T(8,128)(2,1)S(1)}, bf16[1024,128]{1,0:T(8,128)(2,1)S(1)}, u32[]{:S(2)}, u32[]{:S(2)}) collective-permute-start(bf16[1024,128]{1,0:T(8,128)(2,1)S(1)} %slice_bitcast_fusion), channel_id=1, source_target_pairs={{0,24},{8,0},{16,8},{24,16},{1,25},{9,1},{17,9},{25,17},{2,26},{10... | collective-permute-start | bytes 786440 | tf_op jit(solution)/shard_map/forward/ppermute | solution.py:28
  22.5 8.2 %collective-permute-start.1 = (bf16[64,1408]{1,0:T(8,128)(2,1)}, bf16[64,1408]{1,0:T(8,128)(2,1)S(1)}, u32[]{:S(2)}, u32[]{:S(2)}) collective-permute-start(bf16[64,1408]{1,0:T(8,128)(2,1)} %get-tuple-element.31), channel_id=1, source_target_pairs={{0,8},{8,16},{16,24},{24,0},{1,9},{9,17},{17,25},{25,1},{2,10},{10... | collective-permute-start | bytes 540680 | tf_op jit(solution)/shard_map/sums0/ppermute | solution.py:28
  22.5 15.1 %collective-permute-start.4 = (bf16[2,1024,128]{2,1,0:T(8,128)(2,1)S(1)}, bf16[2,1024,128]{2,1,0:T(8,128)(2,1)S(1)}, u32[]{:S(2)}, u32[]{:S(2)}) collective-permute-start(bf16[2,1024,128]{2,1,0:T(8,128)(2,1)S(1)} %collective-permute-done.3.rest_2_.rest_4_), channel_id=1, source_target_pairs={{0,32},{32,0},{64,96},{96,64},{128,160},{160,128},{192,224},{224,1... | collective-permute-start | bytes 1572872 | tf_op jit(solution)/shard_map/swap/ppermute | solution.py:43
  22.5 16.7 %collective-permute-start.6 = (bf16[2,1024,128]{2,1,0:T(8,128)(2,1)S(1)}, bf16[2,1024,128]{2,1,0:T(8,128)(2,1)S(1)}, u32[]{:S(2)}, u32[]{:S(2)}) collective-permute-start(bf16[2,1024,128]{2,1,0:T(8,128)(2,1)S(1)} %collective-permute-done.5.rest_4_.rest_6_), channel_id=1, source_target_pairs={{0,32},{32,0},{64,96},{96,64},{128,160},{160,128},{192,224},{224,1... | collective-permute-start | bytes 1572872 | tf_op jit(solution)/shard_map/swap/ppermute | solution.py:43
  30.7 6.0 %collective-permute-start.2 = (bf16[64,1408]{1,0:T(8,128)(2,1)}, bf16[64,1408]{1,0:T(8,128)(2,1)S(1)}, u32[]{:S(2)}, u32[]{:S(2)}) collective-permute-start(bf16[64,1408]{1,0:T(8,128)(2,1)} %get-tuple-element.32), channel_id=1, source_target_pairs={{0,24},{8,0},{16,8},{24,16},{1,25},{9,1},{17,9},{25,17},{2,26},{10... | collective-permute-start | bytes 540680 | tf_op jit(solution)/shard_map/sums0/ppermute | solution.py:28
  31.2 9.7 %collective-permute-start.9 = (bf16[1024,128]{1,0:T(8,128)(2,1)S(1)}, bf16[1024,128]{1,0:T(8,128)(2,1)S(1)}, u32[]{:S(2)}, u32[]{:S(2)}) collective-permute-start(bf16[1024,128]{1,0:T(8,128)(2,1)S(1)} %collective-permute-done.7.rest_6_.rest_8_), channel_id=1, source_target_pairs={{0,32},{32,0},{64,96},{96,64},{128,160},{160,128},{192,224},{224,1... | collective-permute-start | bytes 786440 | tf_op jit(solution)/shard_map/swap/ppermute | solution.py:43
  31.2 9.6 %collective-permute-start.10 = (bf16[1024,128]{1,0:T(8,128)(2,1)S(1)}, bf16[1024,128]{1,0:T(8,128)(2,1)S(1)}, u32[]{:S(2)}, u32[]{:S(2)}) collective-permute-start(bf16[1024,128]{1,0:T(8,128)(2,1)S(1)} %collective-permute-done.8.rest_7_.rest_9_), channel_id=1, source_target_pairs={{0,32},{32,0},{64,96},{96,64},{128,160},{160,128},{192,224},{224,1... | collective-permute-start | bytes 786440 | tf_op jit(solution)/shard_map/swap/ppermute | solution.py:43
  36.7 15.5 %collective-permute-start.14 = (bf16[64,1408]{1,0:T(8,128)(2,1)}, bf16[64,1408]{1,0:T(8,128)(2,1)S(1)}, u32[]{:S(2)}, u32[]{:S(2)}) collective-permute-start(bf16[64,1408]{1,0:T(8,128)(2,1)} %get-tuple-element.35), channel_id=1, source_target_pairs={{0,16},{8,24},{16,0},{24,8},{1,17},{9,25},{17,1},{25,9},{2,18},{10... | collective-permute-start | bytes 540680 | tf_op jit(solution)/shard_map/sums1/ppermute | solution.py:28
  37.6 16.9 %collective-permute-start.15 = (bf16[64,1408]{1,0:T(8,128)(2,1)}, bf16[64,1408]{1,0:T(8,128)(2,1)S(1)}, u32[]{:S(2)}, u32[]{:S(2)}) collective-permute-start(bf16[64,1408]{1,0:T(8,128)(2,1)} %get-tuple-element.36), channel_id=1, source_target_pairs={{0,8},{8,16},{16,24},{24,0},{1,9},{9,17},{17,25},{25,1},{2,10},{10... | collective-permute-start | bytes 540680 | tf_op jit(solution)/shard_map/sums1/ppermute | solution.py:28
  39.3 15.3 %collective-permute-start.16 = (bf16[64,1408]{1,0:T(8,128)(2,1)}, bf16[64,1408]{1,0:T(8,128)(2,1)S(1)}, u32[]{:S(2)}, u32[]{:S(2)}) collective-permute-start(bf16[64,1408]{1,0:T(8,128)(2,1)} %get-tuple-element.37), channel_id=1, source_target_pairs={{0,24},{8,0},{16,8},{24,16},{1,25},{9,1},{17,9},{25,17},{2,26},{10... | collective-permute-start | bytes 540680 | tf_op jit(solution)/shard_map/sums1/ppermute | solution.py:28
  40.9 0.9 copy-start.6
  41.8 12.7 %copy-start.5 = (bf16[64,1408]{1,0:T(8,128)(2,1)S(1)}, bf16[64,1408]{1,0:T(8,128)(2,1)}, u32[]{:S(2)}) copy-start(bf16[64,1408]{1,0:T(8,128)(2,1)} %get-tuple-element.34.p0) | copy-start | bytes 540676
  50.5 12.8 %collective-permute-start.11 = (bf16[64,1024]{1,0:T(8,128)(2,1)S(1)}, bf16[64,1024]{1,0:T(8,128)(2,1)S(1)}, u32[]{:S(2)}, u32[]{:S(2)}) collective-permute-start(bf16[64,1024]{1,0:T(8,128)(2,1)S(1)} %get-tuple-element.33.a0.before), channel_id=1, source_target_pairs={{0,8},{8,16},{16,24},{24,0},{1,9},{9,17},{17,25},{25,1},{2,10},{10... | collective-permute-start | bytes 393224 | tf_op jit(solution)/shard_map/gather0/ppermute | solution.py:28
  51.0 12.3 %collective-permute-start.12 = (bf16[64,1024]{1,0:T(8,128)(2,1)S(1)}, bf16[64,1024]{1,0:T(8,128)(2,1)S(1)}, u32[]{:S(2)}, u32[]{:S(2)}) collective-permute-start(bf16[64,1024]{1,0:T(8,128)(2,1)S(1)} %get-tuple-element.33.a0.before), channel_id=1, source_target_pairs={{0,16},{8,24},{16,0},{24,8},{1,17},{9,25},{17,1},{25,9},{2,18},{10... | collective-permute-start | bytes 393224 | tf_op jit(solution)/shard_map/gather0/ppermute | solution.py:28
  52.2 11.1 %collective-permute-start.13 = (bf16[64,1024]{1,0:T(8,128)(2,1)S(1)}, bf16[64,1024]{1,0:T(8,128)(2,1)S(1)}, u32[]{:S(2)}, u32[]{:S(2)}) collective-permute-start(bf16[64,1024]{1,0:T(8,128)(2,1)S(1)} %get-tuple-element.33.a0.before), channel_id=1, source_target_pairs={{0,24},{8,0},{16,8},{24,16},{1,25},{9,1},{17,9},{25,17},{2,26},{10... | collective-permute-start | bytes 393224 | tf_op jit(solution)/shard_map/gather0/ppermute | solution.py:28
  54.6 8.7 %copy-start = (bf16[1024,2048]{1,0:T(8,128)(2,1)S(1)}, bf16[1024,2048]{1,0:T(8,128)(2,1)}, u32[]{:S(2)}) copy-start(bf16[1024,2048]{1,0:T(8,128)(2,1)} %w_out.3) | copy-start | bytes 12582916
  66.4 17.2 %collective-permute-start.17 = (bf16[2,256,256]{2,1,0:T(8,128)(2,1)S(1)}, bf16[2,256,256]{2,1,0:T(8,128)(2,1)S(1)}, u32[]{:S(2)}, u32[]{:S(2)}) collective-permute-start(bf16[2,256,256]{2,1,0:T(8,128)(2,1)S(1)} %get-tuple-element.41), channel_id=1, source_target_pairs={{0,4},{1,5},{2,6},{3,7},{4,0},{5,1},{6,2},{7,3},{8,12},{9,13},{10,... | collective-permute-start | bytes 786440 | tf_op jit(solution)/shard_map/x0/ppermute | solution.py:33
  68.6 7.6 %collective-permute-start.21 = (bf16[64,1024]{1,0:T(8,128)(2,1)S(1)}, bf16[64,1024]{1,0:T(8,128)(2,1)S(1)}, u32[]{:S(2)}, u32[]{:S(2)}) collective-permute-start(bf16[64,1024]{1,0:T(8,128)(2,1)S(1)} %attend.3.before.a0), channel_id=1, source_target_pairs={{0,8},{8,16},{16,24},{24,0},{1,9},{9,17},{17,25},{25,1},{2,10},{10... | collective-permute-start | bytes 393224 | tf_op jit(solution)/shard_map/gather1/ppermute | solution.py:28
  68.7 8.9 %collective-permute-start.22 = (bf16[64,1024]{1,0:T(8,128)(2,1)S(1)}, bf16[64,1024]{1,0:T(8,128)(2,1)S(1)}, u32[]{:S(2)}, u32[]{:S(2)}) collective-permute-start(bf16[64,1024]{1,0:T(8,128)(2,1)S(1)} %attend.3.before.a0), channel_id=1, source_target_pairs={{0,16},{8,24},{16,0},{24,8},{1,17},{9,25},{17,1},{25,9},{2,18},{10... | collective-permute-start | bytes 393224 | tf_op jit(solution)/shard_map/gather1/ppermute | solution.py:28
  70.7 6.9 %collective-permute-start.23 = (bf16[64,1024]{1,0:T(8,128)(2,1)S(1)}, bf16[64,1024]{1,0:T(8,128)(2,1)S(1)}, u32[]{:S(2)}, u32[]{:S(2)}) collective-permute-start(bf16[64,1024]{1,0:T(8,128)(2,1)S(1)} %attend.3.before.a0), channel_id=1, source_target_pairs={{0,24},{8,0},{16,8},{24,16},{1,25},{9,1},{17,9},{25,17},{2,26},{10... | collective-permute-start | bytes 393224 | tf_op jit(solution)/shard_map/gather1/ppermute | solution.py:28
  73.4 10.4 %collective-permute-start.18 = (bf16[2,256,256]{2,1,0:T(8,128)(2,1)S(1)}, bf16[2,256,256]{2,1,0:T(8,128)(2,1)S(1)}, u32[]{:S(2)}, u32[]{:S(2)}) collective-permute-start(bf16[2,256,256]{2,1,0:T(8,128)(2,1)S(1)} %get-tuple-element.42), channel_id=1, source_target_pairs={{0,2},{1,3},{2,4},{3,5},{4,6},{5,7},{6,0},{7,1},{8,10},{9,11},{10,... | collective-permute-start | bytes 786440 | tf_op jit(solution)/shard_map/x0/ppermute | solution.py:33
  76.2 12.5 %collective-permute-start.19 = (bf16[2,256,256]{2,1,0:T(8,128)(2,1)S(1)}, bf16[2,256,256]{2,1,0:T(8,128)(2,1)S(1)}, u32[]{:S(2)}, u32[]{:S(2)}) collective-permute-start(bf16[2,256,256]{2,1,0:T(8,128)(2,1)S(1)} %get-tuple-element.43), channel_id=1, source_target_pairs={{0,6},{1,7},{2,0},{3,1},{4,2},{5,3},{6,4},{7,5},{8,14},{9,15},{10,... | collective-permute-start | bytes 786440 | tf_op jit(solution)/shard_map/x0/ppermute | solution.py:33
  80.8 14.8 %collective-permute-start.24 = (bf16[2,256,256]{2,1,0:T(8,128)(2,1)S(1)}, bf16[2,256,256]{2,1,0:T(8,128)(2,1)S(1)}, u32[]{:S(2)}, u32[]{:S(2)}) collective-permute-start(bf16[2,256,256]{2,1,0:T(8,128)(2,1)S(1)} %get-tuple-element.48), channel_id=1, source_target_pairs={{0,4},{1,5},{2,6},{3,7},{4,0},{5,1},{6,2},{7,3},{8,12},{9,13},{10,... | collective-permute-start | bytes 786440 | tf_op jit(solution)/shard_map/x1/ppermute | solution.py:33
  81.7 13.9 %collective-permute-start.25 = (bf16[2,256,256]{2,1,0:T(8,128)(2,1)S(1)}, bf16[2,256,256]{2,1,0:T(8,128)(2,1)S(1)}, u32[]{:S(2)}, u32[]{:S(2)}) collective-permute-start(bf16[2,256,256]{2,1,0:T(8,128)(2,1)S(1)} %get-tuple-element.49), channel_id=1, source_target_pairs={{0,2},{1,3},{2,4},{3,5},{4,6},{5,7},{6,0},{7,1},{8,10},{9,11},{10,... | collective-permute-start | bytes 786440 | tf_op jit(solution)/shard_map/x1/ppermute | solution.py:33
  83.5 12.1 %collective-permute-start.26 = (bf16[2,256,256]{2,1,0:T(8,128)(2,1)S(1)}, bf16[2,256,256]{2,1,0:T(8,128)(2,1)S(1)}, u32[]{:S(2)}, u32[]{:S(2)}) collective-permute-start(bf16[2,256,256]{2,1,0:T(8,128)(2,1)S(1)} %get-tuple-element.50), channel_id=1, source_target_pairs={{0,6},{1,7},{2,0},{3,1},{4,2},{5,3},{6,4},{7,5},{8,14},{9,15},{10,... | collective-permute-start | bytes 786440 | tf_op jit(solution)/shard_map/x1/ppermute | solution.py:33
  89.3 11.5 %collective-permute-start.20 = (bf16[256,256]{1,0:T(8,128)(2,1)S(1)}, bf16[256,256]{1,0:T(8,128)(2,1)S(1)}, u32[]{:S(2)}, u32[]{:S(2)}) collective-permute-start(bf16[256,256]{1,0:T(8,128)(2,1)S(1)} %get-tuple-element.45.before), channel_id=1, source_target_pairs={{0,1},{1,0},{2,3},{3,2},{4,5},{5,4},{6,7},{7,6},{8,9},{9,8},{10,11... | collective-permute-start | bytes 393224 | tf_op jit(solution)/shard_map/z0/ppermute | solution.py:39
  96.3 9.7 %collective-permute-start.27 = (bf16[256,256]{1,0:T(8,128)(2,1)S(1)}, bf16[256,256]{1,0:T(8,128)(2,1)S(1)}, u32[]{:S(2)}, u32[]{:S(2)}) collective-permute-start(bf16[256,256]{1,0:T(8,128)(2,1)S(1)} %get-tuple-element.52), channel_id=1, source_target_pairs={{0,1},{1,0},{2,3},{3,2},{4,5},{5,4},{6,7},{7,6},{8,9},{9,8},{10,11... | collective-permute-start | bytes 393224 | tf_op jit(solution)/shard_map/z1/ppermute | solution.py:39

commit v2 on v1

--- a/solution.py
+++ b/solution.py
@@ -424,7 +424,7 @@
     for h in range(HALVES):
         with jax.named_scope(f"sums{h}"):
             parts.append(
-                [chunks[h]] + [section_shift(chunks[r * HALVES + h], r) for r in (2, 1, 3)]
+                [chunks[h]] + [section_shift(chunks[r * HALVES + h], r) for r in (2, 3, 1)]
             )
     before, attended, gathered = [], [], []
     for h in range(HALVES):
@@ -441,7 +441,7 @@
     for h in range(HALVES):
         *sums, turn = project_out(place, gathered[h], w_out, turn)
         with jax.named_scope(f"x{h}"):
-            pieces = [sums[0]] + [x_shift(sums[r], r) for r in (2, 1, 3)]
+            pieces = [sums[0]] + [x_shift(sums[r], r) for r in (2, 3, 1)]
         send, keep = reduce_pieces(place, send, pieces)
         with jax.named_scope(f"z{h}"):
             arrived = z_swap(send)

time: 108 us -> 107 us (level)
  the two profiles are of different devices: /device:TPU:34 before, /device:TPU:32 now
where the time goes in v2:
time: 107 us
  starting transfers between devices  46.3 us (43%)
  Pallas kernels  33.1 us (31%)
  waiting for transfers between devices  23.9 us (22%)
  local copies, waits for them, and re-layouts  2.04 us (2%)
  other arithmetic  1.15 us (1%)
    ppermute x16, starting transfers between devices, section_shift(): return lax.ppermute(x, 'section', [(i, (i + by) % n) for i in range(n)])  25 us
    pallas_call x2, Pallas kernels, attend(): pl.pallas_call(functools.partial(attention_kernel, half), in_specs=[smem,...  17.3 us
    ppermute x16, waiting for transfers between devices, section_shift(): return lax.ppermute(x, 'section', [(i, (i + by) % n) for i in range(n)])  15.9 us
    ppermute x2, starting transfers between devices, z_swap(): lax.ppermute(x, 'tensor', [(i, i ^ 1) for i in range(lax.axis_size('tenso...  12.2 us
    ppermute x6, starting transfers between devices, x_shift(): lax.ppermute(x, 'tensor', [(i, (i // 2 + by) % n * 2 + i % 2) for i in ra...  8.2 us
    pallas_call x1, Pallas kernels, project(): pl.pallas_call(project_kernel, in_specs=[smem, anywhere, vmem, anywhere,...  7.5 us
    pallas_call x2, Pallas kernels, project_out(): pl.pallas_call(output_kernel, in_specs=[smem] + [vmem] * count + [pl.Bloc...  6.31 us
    ppermute x2, waiting for transfers between devices, z_swap(): lax.ppermute(x, 'tensor', [(i, i ^ 1) for i in range(lax.axis_size('tenso...  4.56 us
  transfers between devices with their start and end apart: 28, of which 8 were waited for; matrix products, arithmetic and copies ran while one was open for 1% of the time, Pallas kernels for 27%

profile of v2, /device:TPU:32, one launch (start us, length us, event | category | flops | bytes accessed | tf_op | source)
XLA Modules:
  0.0 106.8 jit_solution(10641732652193911641)
XLA Ops:
  0.0 1.1 dynamic-slice_bitcast_fusion
  1.1 0.1 pad_maximum_fusion
  1.1 1.7 %collective-permute-start.3 = (bf16[2,1024,128]{2,1,0:T(8,128)(2,1)S(1)}, bf16[2,1024,128]{2,1,0:T(8,128)(2,1)S(1)}, u32[]{:S(2)}, u32[]{:S(2)}) collective-permute-start(bf16[2,1024,128]{2,1,0:T(8,128)(2,1)S(1)} %pad_maximum_fusion), channel_id=1, source_target_pairs={{0,8},{8,16},{16,24},{24,0},{1,9},{9,17},{17,25},{25,1},{2,10},{10... | collective-permute-start | bytes 1572872 | tf_op jit(solution)/shard_map/cache/ppermute | solution.py:28
  2.8 1.7 %collective-permute-start.5 = (bf16[2,1024,128]{2,1,0:T(8,128)(2,1)S(1)}, bf16[2,1024,128]{2,1,0:T(8,128)(2,1)S(1)}, u32[]{:S(2)}, u32[]{:S(2)}) collective-permute-start(bf16[2,1024,128]{2,1,0:T(8,128)(2,1)S(1)} %pad_maximum_fusion), channel_id=1, source_target_pairs={{0,24},{8,0},{16,8},{24,16},{1,25},{9,1},{17,9},{25,17},{2,26},{10... | collective-permute-start | bytes 1572872 | tf_op jit(solution)/shard_map/cache/ppermute | solution.py:28
  4.4 0.7 pad_add_fusion.place
  5.1 7.5 %project.1 = (bf16[64,1408]{1,0:T(8,128)(2,1)}, bf16[64,1408]{1,0:T(8,128)(2,1)}, bf16[64,1408]{1,0:T(8,128)(2,1)}, bf16[64,1408]{1,0:T(8,128)(2,1)}, bf16[64,14...) custom-call(s32[4]{0:T(128)} %pad_add_fusion.place, ...), custom_call_target="tpu_custom_call" | custom-call | flops 2684354560 | bytes 9437184 | tf_op jit(solution)/shard_map/project/pallas_call | solution.py:106
  12.6 2.1 %collective-permute-start = (bf16[64,1408]{1,0:T(8,128)(2,1)}, bf16[64,1408]{1,0:T(8,128)(2,1)S(1)}, u32[]{:S(2)}, u32[]{:S(2)}) collective-permute-start(bf16[64,1408]{1,0:T(8,128)(2,1)} %get-tuple-element.30), channel_id=1, source_target_pairs={{0,16},{8,24},{16,0},{24,8},{1,17},{9,25},{17,1},{25,9},{2,18},{10... | collective-permute-start | bytes 540680 | tf_op jit(solution)/shard_map/sums0/ppermute | solution.py:28
  14.7 1.5 %collective-permute-done.3.rest_2_.rest_4_ = bf16[2,1024,128]{2,1,0:T(8,128)(2,1)S(1)} collective-permute-done((bf16[2,1024,128]{2,1,0:T(8,128)(2,1)S(1)}, bf16[2,1024,128]{2,1,0:T(8,128)(2,1)S(1)}, u32[]{:S(2)}, u32[]{:S(2)}) %collective-permute-start.3) | collective-permute-done | bytes 524320 | tf_op jit(solution)/shard_map/cache/ppermute | solution.py:28
  16.2 0.4 collective-permute-start.7
  16.5 2.0 %collective-permute-done.5.rest_4_.rest_6_ = bf16[2,1024,128]{2,1,0:T(8,128)(2,1)S(1)} collective-permute-done((bf16[2,1024,128]{2,1,0:T(8,128)(2,1)S(1)}, bf16[2,1024,128]{2,1,0:T(8,128)(2,1)S(1)}, u32[]{:S(2)}, u32[]{:S(2)}) %collective-permute-start.5) | collective-permute-done | bytes 524320 | tf_op jit(solution)/shard_map/cache/ppermute | solution.py:28
  18.5 4.0 %collective-permute-start.8 = (bf16[1024,128]{1,0:T(8,128)(2,1)S(1)}, bf16[1024,128]{1,0:T(8,128)(2,1)S(1)}, u32[]{:S(2)}, u32[]{:S(2)}) collective-permute-start(bf16[1024,128]{1,0:T(8,128)(2,1)S(1)} %slice_bitcast_fusion), channel_id=1, source_target_pairs={{0,24},{8,0},{16,8},{24,16},{1,25},{9,1},{17,9},{25,17},{2,26},{10... | collective-permute-start | bytes 786440 | tf_op jit(solution)/shard_map/forward/ppermute | solution.py:28
  22.5 0.1 collective-permute-start.1
  22.6 0.0 collective-permute-done.p1
  22.6 0.5 collective-permute-start.6
  23.1 6.4 %collective-permute-done.1.p2 = bf16[64,1408]{1,0:T(8,128)(2,1)S(1)} collective-permute-done((bf16[64,1408]{1,0:T(8,128)(2,1)}, bf16[64,1408]{1,0:T(8,128)(2,1)S(1)}, u32[]{:S(2)}, u32[]{:S(2)}) %collective-permute-start.1) | collective-permute-done | bytes 180256 | tf_op jit(solution)/shard_map/sums0/ppermute | solution.py:28
  29.6 2.0 %collective-permute-start.2 = (bf16[64,1408]{1,0:T(8,128)(2,1)}, bf16[64,1408]{1,0:T(8,128)(2,1)S(1)}, u32[]{:S(2)}, u32[]{:S(2)}) collective-permute-start(bf16[64,1408]{1,0:T(8,128)(2,1)} %get-tuple-element.32), channel_id=1, source_target_pairs={{0,8},{8,16},{16,24},{24,0},{1,9},{9,17},{17,25},{25,1},{2,10},{10... | collective-permute-start | bytes 540680 | tf_op jit(solution)/shard_map/sums0/ppermute | solution.py:28
  31.6 0.0 collective-permute-done.7.rest_6_.rest_8_
  31.6 0.0 collective-permute-start.9
  31.6 0.0 collective-permute-done.8.rest_7_.rest_9_
  31.6 0.5 collective-permute-start.10
  32.1 0.3 multiply_sine_fusion
  32.4 0.1 pad_maximum_fusion.1
  32.5 3.9 %collective-permute-done.2.p3 = bf16[64,1408]{1,0:T(8,128)(2,1)S(1)} collective-permute-done((bf16[64,1408]{1,0:T(8,128)(2,1)}, bf16[64,1408]{1,0:T(8,128)(2,1)S(1)}, u32[]{:S(2)}, u32[]{:S(2)}) %collective-permute-start.2) | collective-permute-done | bytes 180256 | tf_op jit(solution)/shard_map/sums0/ppermute | solution.py:28
  36.5 1.6 %collective-permute-start.14 = (bf16[64,1408]{1,0:T(8,128)(2,1)}, bf16[64,1408]{1,0:T(8,128)(2,1)S(1)}, u32[]{:S(2)}, u32[]{:S(2)}) collective-permute-start(bf16[64,1408]{1,0:T(8,128)(2,1)} %get-tuple-element.35), channel_id=1, source_target_pairs={{0,16},{8,24},{16,0},{24,8},{1,17},{9,25},{17,1},{25,9},{2,18},{10... | collective-permute-start | bytes 540680 | tf_op jit(solution)/shard_map/sums1/ppermute | solution.py:28
  38.1 0.0 collective-permute-done.4.rest_3_.rest_5_
  38.1 2.0 %collective-permute-start.15 = (bf16[64,1408]{1,0:T(8,128)(2,1)}, bf16[64,1408]{1,0:T(8,128)(2,1)S(1)}, u32[]{:S(2)}, u32[]{:S(2)}) collective-permute-start(bf16[64,1408]{1,0:T(8,128)(2,1)} %get-tuple-element.36), channel_id=1, source_target_pairs={{0,24},{8,0},{16,8},{24,16},{1,25},{9,1},{17,9},{25,17},{2,26},{10... | collective-permute-start | bytes 540680 | tf_op jit(solution)/shard_map/sums1/ppermute | solution.py:28
  40.1 0.0 collective-permute-done.6.rest_5_.rest_7_
  40.1 0.0 collective-permute-start.16
  40.2 0.0 collective-permute-done.9.rest_8_.rest_10_
  40.2 0.0 copy-start.6
  40.2 0.9 copy-done.6
  41.1 8.6 %attend.2 = (bf16[64,1024]{1,0:T(8,128)(2,1)S(1)}, bf16[64,128]{1,0:T(8,128)(2,1)S(1)}, bf16[64,128]{1,0:T(8,128)(2,1)S(1)}) custom-call(s32[4]{0:T(128)S(1)} %copy-done.3, s32[4,128]{1,0:T(4,128)S(1)} %copy-done.4, bf16[64,1408]{1,0:T(8,128)(2,1)S(1)} %copy-done.6, bf16[64,1408]{1,0:T(8,128)(2,1)S(1)} %collective-permute-done.p1, ...), custom_call_target="tpu_custom_call" | custom-call | flops 4294967296 | bytes 6291456 | tf_op jit(solution)/shard_map/attend/pallas_call | solution.py:267
  49.8 1.1 collective-permute-start.11
  50.8 3.7 %collective-permute-start.12 = (bf16[64,1024]{1,0:T(8,128)(2,1)S(1)}, bf16[64,1024]{1,0:T(8,128)(2,1)S(1)}, u32[]{:S(2)}, u32[]{:S(2)}) collective-permute-start(bf16[64,1024]{1,0:T(8,128)(2,1)S(1)} %get-tuple-element.33.a0.before), channel_id=1, source_target_pairs={{0,16},{8,24},{16,0},{24,8},{1,17},{9,25},{17,1},{25,9},{2,18},{10... | collective-permute-start | bytes 393224 | tf_op jit(solution)/shard_map/gather0/ppermute | solution.py:28
  54.5 0.0 collective-permute-done.14.p1
  54.5 0.0 collective-permute-start.13
  54.5 0.0 collective-permute-done.15.p2
  54.5 0.0 copy-start
  54.5 8.6 %attend.3.before.a0 = bf16[64,1024]{1,0:T(8,128)(2,1)S(1)} custom-call(s32[4]{0:T(128)S(1)} %copy-done.3, s32[4,128]{1,0:T(4,128)S(1)} %copy-done.4, bf16[64,1408]{1,0:T(8,128)(2,1)S(1)} %copy-done.5, bf16[64,1408]{1,0:T(8,128)(2,1)S(1)} %collective-permute-done.14.p1, bf16[64,1408]{1,0:T(8,128)(2,1)S(1)} %collective-permute-done.15.p2, ...), custom_call_target="tpu_custom_call" | custom-call | flops 4294967296 | bytes 6291456 | tf_op jit(solution)/shard_map/attend/pallas_call | solution.py:267
  63.2 0.0 collective-permute-done.11.a1
  63.2 0.0 collective-permute-done.13.a3
  63.2 3.1 %project_out.2 = (f32[2,256,256]{2,1,0:T(8,128)S(1)}, bf16[2,256,256]{2,1,0:T(8,128)(2,1)S(1)}, bf16[2,256,256]{2,1,0:T(8,128)(2,1)S(1)}, bf16[2,256,256]{2,1,0:T(8,128)(2,1)S(1)}, f32[8,128]{1,0:T(8,128)S(1)}) custom-call(s32[4]{0:T(128)S(1)} %copy-done.3, bf16[64,1024]{1,0:T(8,128)(2,1)S(1)} %get-tuple-element.33.a0.before, ...), custom_call_target="tpu_custom_call" | custom-call | flops 1073741824 | bytes 6291456 | tf_op jit(solution)/shard_map/project_out/pallas_call | solution.py:321
  66.3 3.1 %collective-permute-start.17 = (bf16[2,256,256]{2,1,0:T(8,128)(2,1)S(1)}, bf16[2,256,256]{2,1,0:T(8,128)(2,1)S(1)}, u32[]{:S(2)}, u32[]{:S(2)}) collective-permute-start(bf16[2,256,256]{2,1,0:T(8,128)(2,1)S(1)} %get-tuple-element.41), channel_id=1, source_target_pairs={{0,4},{1,5},{2,6},{3,7},{4,0},{5,1},{6,2},{7,3},{8,12},{9,13},{10,... | collective-permute-start | bytes 786440 | tf_op jit(solution)/shard_map/x0/ppermute | solution.py:33
  69.4 2.0 %collective-permute-start.21 = (bf16[64,1024]{1,0:T(8,128)(2,1)S(1)}, bf16[64,1024]{1,0:T(8,128)(2,1)S(1)}, u32[]{:S(2)}, u32[]{:S(2)}) collective-permute-start(bf16[64,1024]{1,0:T(8,128)(2,1)S(1)} %attend.3.before.a0), channel_id=1, source_target_pairs={{0,8},{8,16},{16,24},{24,0},{1,9},{9,17},{17,25},{25,1},{2,10},{10... | collective-permute-start | bytes 393224 | tf_op jit(solution)/shard_map/gather1/ppermute | solution.py:28
  71.4 0.0 collective-permute-start.22
  71.4 2.7 %collective-permute-start.23 = (bf16[64,1024]{1,0:T(8,128)(2,1)S(1)}, bf16[64,1024]{1,0:T(8,128)(2,1)S(1)}, u32[]{:S(2)}, u32[]{:S(2)}) collective-permute-start(bf16[64,1024]{1,0:T(8,128)(2,1)S(1)} %attend.3.before.a0), channel_id=1, source_target_pairs={{0,24},{8,0},{16,8},{24,16},{1,25},{9,1},{17,9},{25,17},{2,26},{10... | collective-permute-start | bytes 393224 | tf_op jit(solution)/shard_map/gather1/ppermute | solution.py:28
  74.1 1.1 %collective-permute-start.18 = (bf16[2,256,256]{2,1,0:T(8,128)(2,1)S(1)}, bf16[2,256,256]{2,1,0:T(8,128)(2,1)S(1)}, u32[]{:S(2)}, u32[]{:S(2)}) collective-permute-start(bf16[2,256,256]{2,1,0:T(8,128)(2,1)S(1)} %get-tuple-element.42), channel_id=1, source_target_pairs={{0,6},{1,7},{2,0},{3,1},{4,2},{5,3},{6,4},{7,5},{8,14},{9,15},{10,... | collective-permute-start | bytes 786440 | tf_op jit(solution)/shard_map/x0/ppermute | solution.py:33
  75.3 0.4 collective-permute-done.21.a1
  75.6 0.6 collective-permute-start.19
  76.2 1.7 %collective-permute-done.22.a2 = bf16[64,1024]{1,0:T(8,128)(2,1)S(1)} collective-permute-done((bf16[64,1024]{1,0:T(8,128)(2,1)S(1)}, bf16[64,1024]{1,0:T(8,128)(2,1)S(1)}, u32[]{:S(2)}, u32[]{:S(2)}) %collective-permute-start.22) | collective-permute-done | bytes 131104 | tf_op jit(solution)/shard_map/gather1/ppermute | solution.py:28
  77.9 0.0 collective-permute-done.23.a3
  77.9 3.2 %project_out.3 = (f32[2,256,256]{2,1,0:T(8,128)S(1)}, bf16[2,256,256]{2,1,0:T(8,128)(2,1)S(1)}, bf16[2,256,256]{2,1,0:T(8,128)(2,1)S(1)}, bf16[2,256,256]{2,1,0:T(8,128)(2,1)S(1)}, f32[8,128]{1,0:T(8,128)}) custom-call(s32[4]{0:T(128)S(1)} %copy-done.3, bf16[64,1024]{1,0:T(8,128)(2,1)S(1)} %attend.3.before.a0, ...), custom_call_target="tpu_custom_call" | custom-call | flops 1073741824 | bytes 6291456 | tf_op jit(solution)/shard_map/project_out/pallas_call | solution.py:321
  81.2 0.6 collective-permute-start.24
  81.7 2.8 %collective-permute-start.25 = (bf16[2,256,256]{2,1,0:T(8,128)(2,1)S(1)}, bf16[2,256,256]{2,1,0:T(8,128)(2,1)S(1)}, u32[]{:S(2)}, u32[]{:S(2)}) collective-permute-start(bf16[2,256,256]{2,1,0:T(8,128)(2,1)S(1)} %get-tuple-element.49), channel_id=1, source_target_pairs={{0,6},{1,7},{2,0},{3,1},{4,2},{5,3},{6,4},{7,5},{8,14},{9,15},{10,... | collective-permute-start | bytes 786440 | tf_op jit(solution)/shard_map/x1/ppermute | solution.py:33
  84.5 0.0 collective-permute-done.17.refs_1_
  84.5 0.0 collective-permute-start.26
  84.5 0.0 collective-permute-done.18.refs_2_
  84.5 3.5 %collective-permute-done.19.refs_3_ = bf16[2,256,256]{2,1,0:T(8,128)(2,1)S(1)} collective-permute-done((bf16[2,256,256]{2,1,0:T(8,128)(2,1)S(1)}, bf16[2,256,256]{2,1,0:T(8,128)(2,1)S(1)}, u32[]{:S(2)}, u32[]{:S(2)}) %collective-permute-start.19) | collective-permute-done | bytes 262176 | tf_op jit(solution)/shard_map/x0/ppermute | solution.py:33
  88.0 0.7 reduce_pieces.2
  88.6 6.4 %collective-permute-start.20 = (bf16[256,256]{1,0:T(8,128)(2,1)S(1)}, bf16[256,256]{1,0:T(8,128)(2,1)S(1)}, u32[]{:S(2)}, u32[]{:S(2)}) collective-permute-start(bf16[256,256]{1,0:T(8,128)(2,1)S(1)} %get-tuple-element.45.before), channel_id=1, source_target_pairs={{0,1},{1,0},{2,3},{3,2},{4,5},{5,4},{6,7},{7,6},{8,9},{9,8},{10,11... | collective-permute-start | bytes 393224 | tf_op jit(solution)/shard_map/z0/ppermute | solution.py:39
  95.0 0.7 reduce_pieces.3
  95.7 5.8 %collective-permute-start.27 = (bf16[256,256]{1,0:T(8,128)(2,1)S(1)}, bf16[256,256]{1,0:T(8,128)(2,1)S(1)}, u32[]{:S(2)}, u32[]{:S(2)}) collective-permute-start(bf16[256,256]{1,0:T(8,128)(2,1)S(1)} %get-tuple-element.52), channel_id=1, source_target_pairs={{0,1},{1,0},{2,3},{3,2},{4,5},{5,4},{6,7},{7,6},{8,9},{9,8},{10,11... | collective-permute-start | bytes 393224 | tf_op jit(solution)/shard_map/z1/ppermute | solution.py:39
  101.5 4.6 %collective-permute-done.27.arrived = bf16[256,256]{1,0:T(8,128)(2,1)S(1)} collective-permute-done((bf16[256,256]{1,0:T(8,128)(2,1)S(1)}, bf16[256,256]{1,0:T(8,128)(2,1)S(1)}, u32[]{:S(2)}, u32[]{:S(2)}) %collective-permute-start.27) | collective-permute-done | bytes 131104 | tf_op jit(solution)/shard_map/z1/ppermute | solution.py:39
  106.1 0.7 finish.1
  (24 shorter events, 0.1 us)
Async XLA Ops:
  1.1 15.0 %collective-permute-start.3 = (bf16[2,1024,128]{2,1,0:T(8,128)(2,1)S(1)}, bf16[2,1024,128]{2,1,0:T(8,128)(2,1)S(1)}, u32[]{:S(2)}, u32[]{:S(2)}) collective-permute-start(bf16[2,1024,128]{2,1,0:T(8,128)(2,1)S(1)} %pad_maximum_fusion), channel_id=1, source_target_pairs={{0,8},{8,16},{16,24},{24,0},{1,9},{9,17},{17,25},{25,1},{2,10},{10... | collective-permute-start | bytes 1572872 | tf_op jit(solution)/shard_map/cache/ppermute | solution.py:28
  2.8 15.7 %collective-permute-start.5 = (bf16[2,1024,128]{2,1,0:T(8,128)(2,1)S(1)}, bf16[2,1024,128]{2,1,0:T(8,128)(2,1)S(1)}, u32[]{:S(2)}, u32[]{:S(2)}) collective-permute-start(bf16[2,1024,128]{2,1,0:T(8,128)(2,1)S(1)} %pad_maximum_fusion), channel_id=1, source_target_pairs={{0,24},{8,0},{16,8},{24,16},{1,25},{9,1},{17,9},{25,17},{2,26},{10... | collective-permute-start | bytes 1572872 | tf_op jit(solution)/shard_map/cache/ppermute | solution.py:28
  5.1 35.1 %copy-start.1 = (bf16[2048,128]{1,0:T(8,128)(2,1)S(1)}, bf16[2048,128]{1,0:T(8,128)(2,1)}, u32[]{:S(2)}) copy-start(bf16[2048,128]{1,0:T(8,128)(2,1)} %rest_2_.1) | copy-start | bytes 1572868
  5.1 35.1 %copy-start.2 = (bf16[2048,128]{1,0:T(8,128)(2,1)S(1)}, bf16[2048,128]{1,0:T(8,128)(2,1)}, u32[]{:S(2)}) copy-start(bf16[2048,128]{1,0:T(8,128)(2,1)} %rest_3_.1) | copy-start | bytes 1572868
  5.1 35.1 %copy-start.3 = (s32[4]{0:T(128)S(1)}, s32[4]{0:T(128)}, u32[]{:S(2)}) copy-start(s32[4]{0:T(128)} %pad_add_fusion.place) | copy-start | bytes 52
  5.1 35.1 %copy-start.4 = (s32[4,128]{1,0:T(4,128)S(1)}, s32[4,128]{1,0:T(4,128)}, u32[]{:S(2)}) copy-start(s32[4,128]{1,0:T(4,128)} %mask.3) | copy-start | bytes 6148
  12.6 10.0 %collective-permute-start = (bf16[64,1408]{1,0:T(8,128)(2,1)}, bf16[64,1408]{1,0:T(8,128)(2,1)S(1)}, u32[]{:S(2)}, u32[]{:S(2)}) collective-permute-start(bf16[64,1408]{1,0:T(8,128)(2,1)} %get-tuple-element.30), channel_id=1, source_target_pairs={{0,16},{8,24},{16,0},{24,8},{1,17},{9,25},{17,1},{25,9},{2,18},{10... | collective-permute-start | bytes 540680 | tf_op jit(solution)/shard_map/sums0/ppermute | solution.py:28
  16.2 15.4 %collective-permute-start.7 = (bf16[1024,128]{1,0:T(8,128)(2,1)S(1)}, bf16[1024,128]{1,0:T(8,128)(2,1)S(1)}, u32[]{:S(2)}, u32[]{:S(2)}) collective-permute-start(bf16[1024,128]{1,0:T(8,128)(2,1)S(1)} %slice_bitcast_fusion.1), channel_id=1, source_target_pairs={{0,8},{8,16},{16,24},{24,0},{1,9},{9,17},{17,25},{25,1},{2,10},{10... | collective-permute-start | bytes 786440 | tf_op jit(solution)/shard_map/forward/ppermute | solution.py:28
  18.5 13.1 %collective-permute-start.8 = (bf16[1024,128]{1,0:T(8,128)(2,1)S(1)}, bf16[1024,128]{1,0:T(8,128)(2,1)S(1)}, u32[]{:S(2)}, u32[]{:S(2)}) collective-permute-start(bf16[1024,128]{1,0:T(8,128)(2,1)S(1)} %slice_bitcast_fusion), channel_id=1, source_target_pairs={{0,24},{8,0},{16,8},{24,16},{1,25},{9,1},{17,9},{25,17},{2,26},{10... | collective-permute-start | bytes 786440 | tf_op jit(solution)/shard_map/forward/ppermute | solution.py:28
  22.5 7.1 %collective-permute-start.1 = (bf16[64,1408]{1,0:T(8,128)(2,1)}, bf16[64,1408]{1,0:T(8,128)(2,1)S(1)}, u32[]{:S(2)}, u32[]{:S(2)}) collective-permute-start(bf16[64,1408]{1,0:T(8,128)(2,1)} %get-tuple-element.31), channel_id=1, source_target_pairs={{0,24},{8,0},{16,8},{24,16},{1,25},{9,1},{17,9},{25,17},{2,26},{10... | collective-permute-start | bytes 540680 | tf_op jit(solution)/shard_map/sums0/ppermute | solution.py:28
  22.6 15.5 %collective-permute-start.4 = (bf16[2,1024,128]{2,1,0:T(8,128)(2,1)S(1)}, bf16[2,1024,128]{2,1,0:T(8,128)(2,1)S(1)}, u32[]{:S(2)}, u32[]{:S(2)}) collective-permute-start(bf16[2,1024,128]{2,1,0:T(8,128)(2,1)S(1)} %collective-permute-done.3.rest_2_.rest_4_), channel_id=1, source_target_pairs={{0,32},{32,0},{64,96},{96,64},{128,160},{160,128},{192,224},{224,1... | collective-permute-start | bytes 1572872 | tf_op jit(solution)/shard_map/swap/ppermute | solution.py:43
  22.6 17.5 %collective-permute-start.6 = (bf16[2,1024,128]{2,1,0:T(8,128)(2,1)S(1)}, bf16[2,1024,128]{2,1,0:T(8,128)(2,1)S(1)}, u32[]{:S(2)}, u32[]{:S(2)}) collective-permute-start(bf16[2,1024,128]{2,1,0:T(8,128)(2,1)S(1)} %collective-permute-done.5.rest_4_.rest_6_), channel_id=1, source_target_pairs={{0,32},{32,0},{64,96},{96,64},{128,160},{160,128},{192,224},{224,1... | collective-permute-start | bytes 1572872 | tf_op jit(solution)/shard_map/swap/ppermute | solution.py:43
  29.6 6.9 %collective-permute-start.2 = (bf16[64,1408]{1,0:T(8,128)(2,1)}, bf16[64,1408]{1,0:T(8,128)(2,1)S(1)}, u32[]{:S(2)}, u32[]{:S(2)}) collective-permute-start(bf16[64,1408]{1,0:T(8,128)(2,1)} %get-tuple-element.32), channel_id=1, source_target_pairs={{0,8},{8,16},{16,24},{24,0},{1,9},{9,17},{17,25},{25,1},{2,10},{10... | collective-permute-start | bytes 540680 | tf_op jit(solution)/shard_map/sums0/ppermute | solution.py:28
  31.6 8.6 %collective-permute-start.9 = (bf16[1024,128]{1,0:T(8,128)(2,1)S(1)}, bf16[1024,128]{1,0:T(8,128)(2,1)S(1)}, u32[]{:S(2)}, u32[]{:S(2)}) collective-permute-start(bf16[1024,128]{1,0:T(8,128)(2,1)S(1)} %collective-permute-done.7.rest_6_.rest_8_), channel_id=1, source_target_pairs={{0,32},{32,0},{64,96},{96,64},{128,160},{160,128},{192,224},{224,1... | collective-permute-start | bytes 786440 | tf_op jit(solution)/shard_map/swap/ppermute | solution.py:43
  31.6 8.6 %collective-permute-start.10 = (bf16[1024,128]{1,0:T(8,128)(2,1)S(1)}, bf16[1024,128]{1,0:T(8,128)(2,1)S(1)}, u32[]{:S(2)}, u32[]{:S(2)}) collective-permute-start(bf16[1024,128]{1,0:T(8,128)(2,1)S(1)} %collective-permute-done.8.rest_7_.rest_9_), channel_id=1, source_target_pairs={{0,32},{32,0},{64,96},{96,64},{128,160},{160,128},{192,224},{224,1... | collective-permute-start | bytes 786440 | tf_op jit(solution)/shard_map/swap/ppermute | solution.py:43
  36.5 18.0 %collective-permute-start.14 = (bf16[64,1408]{1,0:T(8,128)(2,1)}, bf16[64,1408]{1,0:T(8,128)(2,1)S(1)}, u32[]{:S(2)}, u32[]{:S(2)}) collective-permute-start(bf16[64,1408]{1,0:T(8,128)(2,1)} %get-tuple-element.35), channel_id=1, source_target_pairs={{0,16},{8,24},{16,0},{24,8},{1,17},{9,25},{17,1},{25,9},{2,18},{10... | collective-permute-start | bytes 540680 | tf_op jit(solution)/shard_map/sums1/ppermute | solution.py:28
  38.1 16.4 %collective-permute-start.15 = (bf16[64,1408]{1,0:T(8,128)(2,1)}, bf16[64,1408]{1,0:T(8,128)(2,1)S(1)}, u32[]{:S(2)}, u32[]{:S(2)}) collective-permute-start(bf16[64,1408]{1,0:T(8,128)(2,1)} %get-tuple-element.36), channel_id=1, source_target_pairs={{0,24},{8,0},{16,8},{24,16},{1,25},{9,1},{17,9},{25,17},{2,26},{10... | collective-permute-start | bytes 540680 | tf_op jit(solution)/shard_map/sums1/ppermute | solution.py:28
  40.1 14.4 %collective-permute-start.16 = (bf16[64,1408]{1,0:T(8,128)(2,1)}, bf16[64,1408]{1,0:T(8,128)(2,1)S(1)}, u32[]{:S(2)}, u32[]{:S(2)}) collective-permute-start(bf16[64,1408]{1,0:T(8,128)(2,1)} %get-tuple-element.37), channel_id=1, source_target_pairs={{0,8},{8,16},{16,24},{24,0},{1,9},{9,17},{17,25},{25,1},{2,10},{10... | collective-permute-start | bytes 540680 | tf_op jit(solution)/shard_map/sums1/ppermute | solution.py:28
  40.2 0.9 copy-start.6
  41.1 13.4 %copy-start.5 = (bf16[64,1408]{1,0:T(8,128)(2,1)S(1)}, bf16[64,1408]{1,0:T(8,128)(2,1)}, u32[]{:S(2)}) copy-start(bf16[64,1408]{1,0:T(8,128)(2,1)} %get-tuple-element.34.p0) | copy-start | bytes 540676
  49.8 13.4 %collective-permute-start.11 = (bf16[64,1024]{1,0:T(8,128)(2,1)S(1)}, bf16[64,1024]{1,0:T(8,128)(2,1)S(1)}, u32[]{:S(2)}, u32[]{:S(2)}) collective-permute-start(bf16[64,1024]{1,0:T(8,128)(2,1)S(1)} %get-tuple-element.33.a0.before), channel_id=1, source_target_pairs={{0,8},{8,16},{16,24},{24,0},{1,9},{9,17},{17,25},{25,1},{2,10},{10... | collective-permute-start | bytes 393224 | tf_op jit(solution)/shard_map/gather0/ppermute | solution.py:28
  50.8 12.4 %collective-permute-start.12 = (bf16[64,1024]{1,0:T(8,128)(2,1)S(1)}, bf16[64,1024]{1,0:T(8,128)(2,1)S(1)}, u32[]{:S(2)}, u32[]{:S(2)}) collective-permute-start(bf16[64,1024]{1,0:T(8,128)(2,1)S(1)} %get-tuple-element.33.a0.before), channel_id=1, source_target_pairs={{0,16},{8,24},{16,0},{24,8},{1,17},{9,25},{17,1},{25,9},{2,18},{10... | collective-permute-start | bytes 393224 | tf_op jit(solution)/shard_map/gather0/ppermute | solution.py:28
  54.5 8.7 %collective-permute-start.13 = (bf16[64,1024]{1,0:T(8,128)(2,1)S(1)}, bf16[64,1024]{1,0:T(8,128)(2,1)S(1)}, u32[]{:S(2)}, u32[]{:S(2)}) collective-permute-start(bf16[64,1024]{1,0:T(8,128)(2,1)S(1)} %get-tuple-element.33.a0.before), channel_id=1, source_target_pairs={{0,24},{8,0},{16,8},{24,16},{1,25},{9,1},{17,9},{25,17},{2,26},{10... | collective-permute-start | bytes 393224 | tf_op jit(solution)/shard_map/gather0/ppermute | solution.py:28
  54.5 8.7 %copy-start = (bf16[1024,2048]{1,0:T(8,128)(2,1)S(1)}, bf16[1024,2048]{1,0:T(8,128)(2,1)}, u32[]{:S(2)}) copy-start(bf16[1024,2048]{1,0:T(8,128)(2,1)} %w_out.3) | copy-start | bytes 12582916
  66.3 18.2 %collective-permute-start.17 = (bf16[2,256,256]{2,1,0:T(8,128)(2,1)S(1)}, bf16[2,256,256]{2,1,0:T(8,128)(2,1)S(1)}, u32[]{:S(2)}, u32[]{:S(2)}) collective-permute-start(bf16[2,256,256]{2,1,0:T(8,128)(2,1)S(1)} %get-tuple-element.41), channel_id=1, source_target_pairs={{0,4},{1,5},{2,6},{3,7},{4,0},{5,1},{6,2},{7,3},{8,12},{9,13},{10,... | collective-permute-start | bytes 786440 | tf_op jit(solution)/shard_map/x0/ppermute | solution.py:33
  69.4 6.2 %collective-permute-start.21 = (bf16[64,1024]{1,0:T(8,128)(2,1)S(1)}, bf16[64,1024]{1,0:T(8,128)(2,1)S(1)}, u32[]{:S(2)}, u32[]{:S(2)}) collective-permute-start(bf16[64,1024]{1,0:T(8,128)(2,1)S(1)} %attend.3.before.a0), channel_id=1, source_target_pairs={{0,8},{8,16},{16,24},{24,0},{1,9},{9,17},{17,25},{25,1},{2,10},{10... | collective-permute-start | bytes 393224 | tf_op jit(solution)/shard_map/gather1/ppermute | solution.py:28
  71.4 6.5 %collective-permute-start.22 = (bf16[64,1024]{1,0:T(8,128)(2,1)S(1)}, bf16[64,1024]{1,0:T(8,128)(2,1)S(1)}, u32[]{:S(2)}, u32[]{:S(2)}) collective-permute-start(bf16[64,1024]{1,0:T(8,128)(2,1)S(1)} %attend.3.before.a0), channel_id=1, source_target_pairs={{0,16},{8,24},{16,0},{24,8},{1,17},{9,25},{17,1},{25,9},{2,18},{10... | collective-permute-start | bytes 393224 | tf_op jit(solution)/shard_map/gather1/ppermute | solution.py:28
  71.4 6.5 %collective-permute-start.23 = (bf16[64,1024]{1,0:T(8,128)(2,1)S(1)}, bf16[64,1024]{1,0:T(8,128)(2,1)S(1)}, u32[]{:S(2)}, u32[]{:S(2)}) collective-permute-start(bf16[64,1024]{1,0:T(8,128)(2,1)S(1)} %attend.3.before.a0), channel_id=1, source_target_pairs={{0,24},{8,0},{16,8},{24,16},{1,25},{9,1},{17,9},{25,17},{2,26},{10... | collective-permute-start | bytes 393224 | tf_op jit(solution)/shard_map/gather1/ppermute | solution.py:28
  74.1 10.4 %collective-permute-start.18 = (bf16[2,256,256]{2,1,0:T(8,128)(2,1)S(1)}, bf16[2,256,256]{2,1,0:T(8,128)(2,1)S(1)}, u32[]{:S(2)}, u32[]{:S(2)}) collective-permute-start(bf16[2,256,256]{2,1,0:T(8,128)(2,1)S(1)} %get-tuple-element.42), channel_id=1, source_target_pairs={{0,6},{1,7},{2,0},{3,1},{4,2},{5,3},{6,4},{7,5},{8,14},{9,15},{10,... | collective-permute-start | bytes 786440 | tf_op jit(solution)/shard_map/x0/ppermute | solution.py:33
  75.6 12.4 %collective-permute-start.19 = (bf16[2,256,256]{2,1,0:T(8,128)(2,1)S(1)}, bf16[2,256,256]{2,1,0:T(8,128)(2,1)S(1)}, u32[]{:S(2)}, u32[]{:S(2)}) collective-permute-start(bf16[2,256,256]{2,1,0:T(8,128)(2,1)S(1)} %get-tuple-element.43), channel_id=1, source_target_pairs={{0,2},{1,3},{2,4},{3,5},{4,6},{5,7},{6,0},{7,1},{8,10},{9,11},{10,... | collective-permute-start | bytes 786440 | tf_op jit(solution)/shard_map/x0/ppermute | solution.py:33
  81.2 13.9 %collective-permute-start.24 = (bf16[2,256,256]{2,1,0:T(8,128)(2,1)S(1)}, bf16[2,256,256]{2,1,0:T(8,128)(2,1)S(1)}, u32[]{:S(2)}, u32[]{:S(2)}) collective-permute-start(bf16[2,256,256]{2,1,0:T(8,128)(2,1)S(1)} %get-tuple-element.48), channel_id=1, source_target_pairs={{0,4},{1,5},{2,6},{3,7},{4,0},{5,1},{6,2},{7,3},{8,12},{9,13},{10,... | collective-permute-start | bytes 786440 | tf_op jit(solution)/shard_map/x1/ppermute | solution.py:33
  81.7 13.3 %collective-permute-start.25 = (bf16[2,256,256]{2,1,0:T(8,128)(2,1)S(1)}, bf16[2,256,256]{2,1,0:T(8,128)(2,1)S(1)}, u32[]{:S(2)}, u32[]{:S(2)}) collective-permute-start(bf16[2,256,256]{2,1,0:T(8,128)(2,1)S(1)} %get-tuple-element.49), channel_id=1, source_target_pairs={{0,6},{1,7},{2,0},{3,1},{4,2},{5,3},{6,4},{7,5},{8,14},{9,15},{10,... | collective-permute-start | bytes 786440 | tf_op jit(solution)/shard_map/x1/ppermute | solution.py:33
  84.5 10.5 %collective-permute-start.26 = (bf16[2,256,256]{2,1,0:T(8,128)(2,1)S(1)}, bf16[2,256,256]{2,1,0:T(8,128)(2,1)S(1)}, u32[]{:S(2)}, u32[]{:S(2)}) collective-permute-start(bf16[2,256,256]{2,1,0:T(8,128)(2,1)S(1)} %get-tuple-element.50), channel_id=1, source_target_pairs={{0,2},{1,3},{2,4},{3,5},{4,6},{5,7},{6,0},{7,1},{8,10},{9,11},{10,... | collective-permute-start | bytes 786440 | tf_op jit(solution)/shard_map/x1/ppermute | solution.py:33
  88.6 12.8 %collective-permute-start.20 = (bf16[256,256]{1,0:T(8,128)(2,1)S(1)}, bf16[256,256]{1,0:T(8,128)(2,1)S(1)}, u32[]{:S(2)}, u32[]{:S(2)}) collective-permute-start(bf16[256,256]{1,0:T(8,128)(2,1)S(1)} %get-tuple-element.45.before), channel_id=1, source_target_pairs={{0,1},{1,0},{2,3},{3,2},{4,5},{5,4},{6,7},{7,6},{8,9},{9,8},{10,11... | collective-permute-start | bytes 393224 | tf_op jit(solution)/shard_map/z0/ppermute | solution.py:39
  95.7 10.4 %collective-permute-start.27 = (bf16[256,256]{1,0:T(8,128)(2,1)S(1)}, bf16[256,256]{1,0:T(8,128)(2,1)S(1)}, u32[]{:S(2)}, u32[]{:S(2)}) collective-permute-start(bf16[256,256]{1,0:T(8,128)(2,1)S(1)} %get-tuple-element.52), channel_id=1, source_target_pairs={{0,1},{1,0},{2,3},{3,2},{4,5},{5,4},{6,7},{7,6},{8,9},{9,8},{10,11... | collective-permute-start | bytes 393224 | tf_op jit(solution)/shard_map/z1/ppermute | solution.py:39
